TPU v7x, 512 devices: a whole 4x8x8 slice. The times are simulated.
512 devices in a mesh: seq: 64 (over z, y_hi, x), grp: 8 (over y_lo, core).
Axes of the slice: x: 4, y: 8 (y_hi: 2, y_lo: 4; y = y_hi * 4 + y_lo), z: 8, core: 2. Of those that a mesh axis runs over, the one named last changes fastest.
Arguments:
- inner_input: bfloat16 [65536, 4096], P(('seq', 'grp')), may hold values from -6 to 6
- inner_gate: bfloat16 [65536, 4096], P(('seq', 'grp')), may hold values from -6 to 6
- conv_weight: float32 [2, 4, 4096], P(None, None, 'grp'), may hold values from -3 to 3
- conv_bias: float32 [2, 4096], P(None, 'grp'), may hold values from -1.5 to 0.5
- proj_weight: bfloat16 [2, 4096, 160], P(None, 'grp'), may hold values from -0.0625 to 0.0625
- step_weight: bfloat16 [2, 128, 4096], P(None, None, 'grp'), may hold values from -0.5 to 0.5
- step_bias: float32 [2, 4096], P(None, 'grp'), may hold values from -12 to 1
- decay_rate: float32 [2, 16, 4096], P(None, None, 'grp'), may hold values from 0.02 to 0.1
- skip_gain: float32 [2, 4096], P(None, 'grp'), may hold values from 0.5 to 1.5
Outputs:
- gated: bfloat16 [65536, 4096], P(('seq', 'grp'))
All inputs are finite; a program needn't handle non-finite values.
Results may differ from a plain program's by a relative error of at most 0.012.
Values may be sent and summed in bfloat16 or wider, within the bound.
A program may use at most 128 MiB of HBM per device.

v0:
```python
import math

import jax
import jax.numpy as jnp
from jax import lax
from jax.sharding import PartitionSpec as P


def with_halo(cells, sides, width):
    for axis, dim in sides:
        count = lax.axis_size(axis)
        ends = count - 1
        head = lax.slice_in_dim(cells, 0, width, axis=dim)
        tail = lax.slice_in_dim(cells, cells.shape[dim] - width, cells.shape[dim], axis=dim)
        cells = jnp.concatenate(
            [
                lax.ppermute(tail, axis, [(i, (i + 1) % count) for i in range(ends)]),
                cells,
                lax.ppermute(head, axis, [((i + 1) % count, i) for i in range(ends)]),
            ],
            axis=dim,
        )
    return cells


def carried_in(value, axis, combine, identity, reverse):
    size, here = (lax.axis_size(axis), lax.axis_index(axis))
    everything = jax.tree.map(lambda part: lax.all_gather(part, axis), value)
    start = jax.tree.map(
        lambda part, zero: jnp.broadcast_to(jnp.asarray(zero, part.dtype), part.shape),
        value,
        identity,
    )

    def turn(k, before):
        at = size - 1 - k if reverse else k
        reached = at > here if reverse else at < here
        new = combine(before, jax.tree.map(lambda part: part[at], everything))
        return jax.tree.map(lambda a, b: jnp.where(reached, a, b), new, before)

    return lax.fori_loop(0, size, turn, start)


def combine_pairs(earlier, later):
    return (earlier[0] * later[0], later[0] * earlier[1] + later[1])


def local_scan(activation, step_size, in_map, out_map, rates):
    row_count, width = activation.shape
    states = rates.shape[0]
    block_rows = math.gcd(row_count, 64)
    block_count = row_count // block_rows
    drive = step_size * activation.astype(jnp.float32)

    def advance(carried, pieces):
        step_rows, drive_rows, in_rows, out_rows = pieces
        elapsed = jnp.cumsum(step_rows, axis=0)
        centred = elapsed - 0.5 * elapsed[-1][None]
        terms = (
            jnp.exp(rates[None] * centred[:, None, :])
            * drive_rows[:, None, :]
            * in_rows[:, :, None]
        )
        summed = jnp.cumsum(terms, axis=0)
        history = (
            jnp.exp(-rates[None] * centred[:, None, :]) * summed
            + jnp.exp(-rates[None] * elapsed[:, None, :]) * carried[None]
        )
        return (history[-1], jnp.sum(out_rows[:, :, None] * history, axis=1))

    pieces = (
        step_size.reshape(block_count, block_rows, width),
        drive.reshape(block_count, block_rows, width),
        in_map.reshape(block_count, block_rows, states),
        out_map.reshape(block_count, block_rows, states),
    )
    last_state, outputs = lax.scan(advance, jnp.zeros((states, width), jnp.float32), pieces)
    return (outputs.reshape(row_count, width), last_state)


def local(
    inner_input,
    inner_gate,
    conv_weight,
    conv_bias,
    proj_weight,
    step_weight,
    step_bias,
    decay_rate,
    skip_gain,
):
    inputs_rows, gate_rows = (
        lax.all_to_all(inner_input, "grp", split_axis=1, concat_axis=0, tiled=True),
        lax.all_to_all(inner_gate, "grp", split_axis=1, concat_axis=0, tiled=True),
    )
    row_count = inputs_rows.shape[0]
    kernel = conv_weight.shape[1]
    low_rank = step_weight.shape[1]
    states = decay_rate.shape[1]
    padded = with_halo(inputs_rows, (("seq", 0),), kernel - 1).astype(jnp.float32)
    activations = []
    partials = []
    for branch in range(2):
        summed = jnp.zeros((row_count, inputs_rows.shape[1]), jnp.float32) + conv_bias[branch][None]
        for position in range(kernel):
            offset = position if branch == 0 else 2 * (kernel - 1) - position
            summed = (
                summed + conv_weight[branch, position][None] * padded[offset : offset + row_count]
            )
        activation = jax.nn.silu(summed).astype(jnp.bfloat16)
        activations.append(activation)
        partials.append(
            jnp.dot(activation, proj_weight[branch], preferred_element_type=jnp.float32)
        )
    forward_sum, reverse_sum = lax.psum((partials[0], partials[1]), "grp")
    results = []
    for branch, summed in ((0, forward_sum), (1, reverse_sum)):
        projected = summed.astype(jnp.bfloat16)
        step_size = jax.nn.softplus(
            jnp.dot(
                projected[:, :low_rank], step_weight[branch], preferred_element_type=jnp.float32
            )
            + step_bias[branch][None]
        )
        in_map = projected[:, low_rank : low_rank + states].astype(jnp.float32)
        out_map = projected[:, low_rank + states :].astype(jnp.float32)
        activation = activations[branch]
        if branch == 1:
            step_size = jnp.flip(step_size, 0)
            in_map = jnp.flip(in_map, 0)
            out_map = jnp.flip(out_map, 0)
            activation = jnp.flip(activation, 0)
        rates = decay_rate[branch]
        local_part, last_state = local_scan(activation, step_size, in_map, out_map, rates)
        elapsed = jnp.cumsum(step_size, axis=0)
        decay_total = jnp.exp(-rates * elapsed[-1][None])
        results.append((local_part, last_state, decay_total, elapsed, out_map, activation))
    identity = (jnp.ones_like(results[0][2]), jnp.zeros_like(results[0][1]))
    forward_carry = carried_in(
        (results[0][2], results[0][1]), "seq", combine_pairs, identity, False
    )[1]
    reverse_carry = carried_in(
        (results[1][2], results[1][1]), "seq", combine_pairs, identity, True
    )[1]
    outputs = []
    for branch, carried in ((0, forward_carry), (1, reverse_carry)):
        local_part, last_state, decay_total, elapsed, out_map, activation = results[branch]
        rates = decay_rate[branch]
        entering = jnp.sum(
            out_map[:, :, None] * jnp.exp(-rates[None] * elapsed[:, None, :]) * carried[None],
            axis=1,
        )
        branch_out = (
            local_part + entering + skip_gain[branch][None] * activation.astype(jnp.float32)
        )
        if branch == 1:
            branch_out = jnp.flip(branch_out, 0)
        outputs.append(branch_out)
    mixed = (outputs[0] + outputs[1]).astype(jnp.bfloat16)
    gated = (mixed.astype(jnp.float32) * jax.nn.silu(gate_rows.astype(jnp.float32))).astype(
        jnp.bfloat16
    )
    return lax.all_to_all(gated, "grp", split_axis=0, concat_axis=1, tiled=True)


def solution(mesh):
    placed = (
        P(("seq", "grp"), None),
        P(("seq", "grp"), None),
        P(None, None, "grp"),
        P(None, "grp"),
        P(None, "grp", None),
        P(None, None, "grp"),
        P(None, "grp"),
        P(None, None, "grp"),
        P(None, "grp"),
    )
    return jax.shard_map(
        local, mesh=mesh, in_specs=placed, out_specs=P(("seq", "grp"), None), check_vma=False
    )
```

profile of v0, /device:TPU:1, one launch (start us, length us, event | category | flops | bytes accessed | tf_op | source)
XLA Modules:
  0.0 921.1 jit_solution(888396495983538816)
XLA Ops:
  6.5 2.3 copy.74
  8.9 10.3 %all-to-all-start = ((bf16[128,8,512]{2,0,1:T(8,128)(2,1)}), bf16[128,8,512]{2,0,1:T(8,128)(2,1)S(1)}, u32[]{:S(2)}, u32[]{:S(2)}) async-start(bf16[128,8,512]{2,0,1:T(8,128)(2,1)} %bitcast.163), calls=%async_computation | async-start | bytes 2097152 | tf_op jit(solution)/shard_map/all_to_all | solution.py:93
  19.3 25.7 %all-to-all-done = bf16[128,8,512]{2,0,1:T(8,128)(2,1)S(1)} async-done(((bf16[128,8,512]{2,0,1:T(8,128)(2,1)}), bf16[128,8,512]{2,0,1:T(8,128)(2,1)S(1)}, u32[]{:S(2)}, u32[]{:S(2)}) %all-to-all-start) | async-done | bytes 1048608 | tf_op jit(solution)/shard_map/all_to_all | solution.py:93
  47.6 3.0 collective-permute-done.1
  52.2 2.7 multiply_convert_fusion.1
  56.4 57.8 %all-reduce.2 = (bf16[1024,160]{0,1:T(8,128)(2,1)}, bf16[1024,160]{0,1:T(8,128)(2,1)S(1)}) all-reduce(f32[1024,160]{0,1:T(8,128)S(1)} %fusion.52, f32[1024,160]{0,1:T(8,128)S(1)} %fusion.54), channel_id=1, replica_groups=mesh['seq'=64,'grp'=8] {'grp'}, use_global_device_ids=true, to_apply=%region_11.12 | all-reduce | flops 327680 | bytes 1966080 | tf_op jit(solution)/shard_map/psum | solution.py:115
  114.2 2.6 compare_select_fusion.1
  121.2 2.7 compare_select_fusion
  123.8 13.7 %rev.18 = f32[1024,512]{1,0:T(8,128)S(1)} reverse(f32[1024,512]{1,0:T(8,128)} %compare_select_fusion), dimensions={0} | reverse | bytes 4194304 | tf_op jit(solution)/shard_map/jit(_flip)/rev | solution.py:129
  144.5 3.3 convert_multiply_fusion.3
  152.7 87.0 %while.56 = (s32[]{:T(128)}, f32[16,512]{1,0:T(8,128)}, f32[16,64,512]{2,1,0:T(8,128)}, f32[1,16,512]{2,1,0:T(8,128)}, f32[16,64,512]{2,1,0:T(8,128)}, /*index=5...) while((s32[]{:T(128)}, f32[16,512]{1,0:T(8,128)}, ...), condition=%wide.region_5.6_spmd, body=%wide.region_1.5_spmd.sunk | while | flops 40337920 | bytes 4127353 | solution.py:77
  154.7 2.2 multiply_reduce_fusion.6
  160.1 2.2 multiply_reduce_fusion.6
  165.5 2.2 multiply_reduce_fusion.6
  171.0 2.2 multiply_reduce_fusion.6
  176.4 2.2 multiply_reduce_fusion.6
  187.3 2.2 multiply_reduce_fusion.6
  192.7 2.2 multiply_reduce_fusion.6
  198.2 2.2 multiply_reduce_fusion.6
  203.6 2.2 multiply_reduce_fusion.6
  209.0 2.2 multiply_reduce_fusion.6
  214.5 2.2 multiply_reduce_fusion.6
  219.9 2.2 multiply_reduce_fusion.6
  225.4 2.2 multiply_reduce_fusion.6
  230.8 2.2 multiply_reduce_fusion.6
  236.2 2.2 multiply_reduce_fusion.6
  239.8 15.5 %rev.19 = bf16[1024,512]{1,0:T(8,128)(2,1)} reverse(bf16[1024,512]{1,0:T(8,128)(2,1)} %copy-done.1), dimensions={0} | reverse | bytes 2097152 | tf_op jit(solution)/shard_map/jit(_flip)/rev | solution.py:132
  258.4 2.9 convert_multiply_fusion.1
  263.9 86.1 %while.57 = (s32[]{:T(128)}, f32[16,512]{1,0:T(8,128)}, f32[16,64,512]{2,1,0:T(8,128)}, f32[1,16,512]{2,1,0:T(8,128)}, f32[16,64,512]{2,1,0:T(8,128)S(1)}, /*ind...) while((s32[]{:T(128)}, f32[16,512]{1,0:T(8,128)}, ...), condition=%wide.region_16.17_spmd, body=%wide.region_12.16_spmd.sunk | while | flops 40337920 | bytes 4127353 | solution.py:77
  265.8 2.2 multiply_reduce_fusion.7
  271.2 2.2 multiply_reduce_fusion.7
  276.6 2.2 multiply_reduce_fusion.7
  281.9 2.2 multiply_reduce_fusion.7
  319.5 2.2 multiply_reduce_fusion.7
  350.0 2.3 copy.73
  352.3 6.3 all-to-all-start.1
  359.2 21.0 %all-gather.11.cloned.1.call-done = f32[1024,512]{1,0:T(8,128)} async-done(((f32[16,512]{1,0:T(8,128)}), f32[1024,512]{1,0:T(8,128)}) %all-gather.11.cloned.1.call-update) | async-done | bytes 2097168 | tf_op jit(solution)/shard_map/all_gather | solution.py:28
  380.2 133.8 %all-gather.7.cloned.1.call-done = f32[64,16,512]{2,1,0:T(8,128)} async-done(((f32[1,16,512]{2,1,0:T(8,128)}), f32[64,16,512]{2,1,0:T(8,128)}) %all-gather.7.cloned.1.call-update) | async-done | bytes 2097168 | tf_op jit(solution)/shard_map/all_gather | solution.py:28
  513.9 52.0 %while.58 = (s32[]{:T(128)}, f32[16,512]{1,0:T(8,128)S(1)}, s32[]{:T(128)}, f32[64,16,512]{2,1,0:T(8,128)}, f32[64,16,512]{2,1,0:T(8,128)}, /*index=5*/s32[]{:T(128)}, s32[]{:T(128)}) while((s32[]{:T(128)}, f32[16,512]{1,0:T(8,128)S(1)}, s32[]{:T(128)}, f32[64,16,512]{2,1,0:T(8,128)}, f32[64,16,512]{2,1,0:T(8,128)}, ...), condition=%wide.region_9.10_spmd.clone, body=%wide.region_8.9_spmd.clone.sunk | while | flops 32772 | bytes 131173 | solution.py:41
  565.9 82.0 %all-gather.13.cloned.1.call-done = f32[1024,512]{1,0:T(8,128)} async-done(((f32[16,512]{1,0:T(8,128)}), f32[1024,512]{1,0:T(8,128)}) %all-gather.13.cloned.1.call-update) | async-done | bytes 2097168 | tf_op jit(solution)/shard_map/all_gather | solution.py:28
  648.0 133.9 %all-gather.9.cloned.1.call-done = f32[64,16,512]{2,1,0:T(8,128)} async-done(((f32[1,16,512]{2,1,0:T(8,128)}), f32[64,16,512]{2,1,0:T(8,128)}) %all-gather.9.cloned.1.call-update) | async-done | bytes 2097168 | tf_op jit(solution)/shard_map/all_gather | solution.py:28
  781.8 52.4 %while.59 = (s32[]{:T(128)}, f32[16,512]{1,0:T(8,128)S(1)}, s32[]{:T(128)}, f32[64,16,512]{2,1,0:T(8,128)}, f32[64,16,512]{2,1,0:T(8,128)}, /*index=5*/s32[]{:T(128)}, s32[]{:T(128)}, s32[]{:T(128)}, s32[]{:T(128)}) while((s32[]{:T(128)}, f32[16,512]{1,0:T(8,128)S(1)}, s32[]{:T(128)}, f32[64,16,512]{2,1,0:T(8,128)}, ...), condition=%wide.region_20.21_spmd.clone, body=%wide.region_19.20_spmd.clone.sunk | while | flops 32776 | bytes 131235 | solution.py:41
  834.3 11.2 %multiply_reduce_fusion.2 = f32[1024,512]{1,0:T(8,128)S(1)} fusion(f32[16,512]{1,0:T(8,128)S(1)} %get-tuple-element.396, f32[1024,512]{1,0:T(8,128)S(1)} %bitcast.212, f32[16,512]{1,0:T(8,128)S(1)} %copy-done.12, f32[1024,16]{1,0:T(8,128)} %bitcast.219), kind=kLoop, calls=%fused_computation.44 | loop fusion | flops 33030144 | bytes 4325376 | tf_op jit(solution)/shard_map/reduce_sum | solution.py:149
  845.5 3.5 fusion.27
  849.1 13.7 %rev.22 = f32[1024,512]{1,0:T(8,128)S(1)} reverse(f32[1024,512]{1,0:T(8,128)} %fusion.27), dimensions={0} | reverse | bytes 4194304 | tf_op jit(solution)/shard_map/jit(_flip)/rev | solution.py:157
  862.7 12.6 %multiply_reduce_fusion.3 = f32[1024,512]{1,0:T(8,128)} fusion(f32[16,512]{1,0:T(8,128)S(1)} %get-tuple-element.393, f32[1024,512]{1,0:T(8,128)} %bitcast.210, f32[16,512]{1,0:T(8,128)S(1)} %copy-done.11, f32[1024,16]{1,0:T(8,128)} %bitcast.217), kind=kLoop, calls=%fused_computation.45 | loop fusion | flops 33030144 | bytes 4325376 | tf_op jit(solution)/shard_map/reduce_sum | solution.py:149
  875.3 3.5 fusion.48
  878.8 34.6 %all_to_all.51 = bf16[8,128,512]{2,1,0:T(8,128)(2,1)S(1)} all-to-all(bf16[8,128,512]{2,1,0:T(8,128)(2,1)S(1)} %bitcast.204), channel_id=1, replica_groups=mesh['seq'=64,'grp'=8] {'grp'}, dimensions={0} | all-to-all | bytes 2097152 | tf_op jit(solution)/shard_map/all_to_all | solution.py:163
  (456 shorter events, 258.5 us)
Async XLA Ops:
  6.5 12.7 %copy-start.16 = (f32[2,512]{1,0:T(2,128)S(1)}, f32[2,512]{1,0:T(2,128)}, u32[]{:S(2)}) copy-start(f32[2,512]{1,0:T(2,128)} %param.20) | copy-start | bytes 12292
  6.5 12.7 %copy-start.13 = (f32[2,4,512]{2,1,0:T(4,128)S(1)}, f32[2,4,512]{2,1,0:T(4,128)}, u32[]{:S(2)}) copy-start(f32[2,4,512]{2,1,0:T(4,128)} %param.19) | copy-start | bytes 49156
  6.5 41.0 %copy-start.17 = (f32[2,512]{1,0:T(2,128)S(1)}, f32[2,512]{1,0:T(2,128)}, u32[]{:S(2)}) copy-start(f32[2,512]{1,0:T(2,128)} %param.23) | copy-start | bytes 12292
  8.9 36.1 %all-to-all-start = ((bf16[128,8,512]{2,0,1:T(8,128)(2,1)}), bf16[128,8,512]{2,0,1:T(8,128)(2,1)S(1)}, u32[]{:S(2)}, u32[]{:S(2)}) async-start(bf16[128,8,512]{2,0,1:T(8,128)(2,1)} %bitcast.163), calls=%async_computation | async-start | bytes 2097152 | tf_op jit(solution)/shard_map/all_to_all | solution.py:93
  19.2 361.0 %all-gather.11.cloned.1.call-start = ((), (), s32[]{:S(2)}) async-start(), calls=%async_computation.5 | async-start | bytes 2129920 | tf_op jit(solution)/shard_map/all_gather | solution.py:28
  45.0 2.6 collective-permute-start
  46.3 4.4 collective-permute-start.1
  52.2 2.7 copy-start.7
  54.9 1.0 copy-start.1
  54.9 59.2 %copy-start.19 = (bf16[2,128,512]{2,1,0:T(8,128)(2,1)S(1)}, bf16[2,128,512]{2,1,0:T(8,128)(2,1)}, u32[]{:S(2)}) copy-start(bf16[2,128,512]{2,1,0:T(8,128)(2,1)} %param.22) | copy-start | bytes 786436
  114.2 2.6 copy-start.15
  118.4 1.3 copy-start.14
  118.4 2.8 copy-start.20
  119.6 1.6 copy-start.3
  138.8 1.3 copy-start.2
  142.0 2.5 copy-start.6
  143.2 1.3 copy-start.4
  144.5 5.3 copy-start.10
  239.7 15.5 %copy-start.9 = (f32[1024,16]{0,1:T(8,128)S(1)}, f32[1024,16]{0,1:T(8,128)}, u32[]{:S(2)}) copy-start(f32[1024,16]{0,1:T(8,128)} %get-tuple-element.584) | copy-start | bytes 196612
  239.7 17.1 %copy-start.8 = (f32[1024,16]{0,1:T(8,128)S(1)}, f32[1024,16]{0,1:T(8,128)}, u32[]{:S(2)}) copy-start(f32[1024,16]{0,1:T(8,128)} %get-tuple-element.583) | copy-start | bytes 196612
  239.8 274.2 %all-gather.7.cloned.1.call-start = ((), (), s32[]{:S(2)}) async-start(), calls=%async_computation.3 | async-start | bytes 2129920 | tf_op jit(solution)/shard_map/all_gather | solution.py:28
  261.4 386.5 %all-gather.13.cloned.1.call-start = ((), (), s32[]{:S(2)}) async-start(), calls=%async_computation.6 | async-start | bytes 2129920 | tf_op jit(solution)/shard_map/all_gather | solution.py:28
  350.0 8.6 copy-start.18
  352.3 481.9 %copy-start.5 = (f32[512,8,128]{0,2,1:T(8,128)S(1)}, f32[512,8,128]{0,2,1:T(8,128)}, u32[]{:S(2)}) copy-start(f32[512,8,128]{0,2,1:T(8,128)} %copy-done.4) | copy-start | bytes 6291460
  352.3 482.0 %copy-start.12 = (f32[16,512]{1,0:T(8,128)S(1)}, f32[16,512]{1,0:T(8,128)}, u32[]{:S(2)}) copy-start(f32[16,512]{1,0:T(8,128)} %get-tuple-element.586) | copy-start | bytes 98308
  352.3 523.0 %all-to-all-start.1 = ((bf16[128,8,512]{2,0,1:T(8,128)(2,1)}), bf16[128,8,512]{2,0,1:T(8,128)(2,1)}, u32[]{:S(2)}, u32[]{:S(2)}) async-start(bf16[128,8,512]{2,0,1:T(8,128)(2,1)} %bitcast.162), calls=%async_computation.1 | async-start | bytes 2097152 | tf_op jit(solution)/shard_map/all_to_all | solution.py:94
  358.6 423.2 %all-gather.9.cloned.1.call-start = ((), (), s32[]{:S(2)}) async-start(), calls=%async_computation.4 | async-start | bytes 2129920 | tf_op jit(solution)/shard_map/all_gather | solution.py:28
  834.3 11.3 %copy-start = (bf16[1024,512]{1,0:T(8,128)(2,1)S(1)}, bf16[1024,512]{1,0:T(8,128)(2,1)}, u32[]{:S(2)}) copy-start(bf16[1024,512]{1,0:T(8,128)(2,1)} %rev.19) | copy-start | bytes 3145732
  849.1 13.7 %copy-start.11 = (f32[16,512]{1,0:T(8,128)S(1)}, f32[16,512]{1,0:T(8,128)}, u32[]{:S(2)}) copy-start(f32[16,512]{1,0:T(8,128)} %get-tuple-element.585) | copy-start | bytes 98308
Sparse Core Ops, SparseCore 0:
  239.9 140.2 all-gather.10
  384.6 129.2 all-gather.6
  518.4 129.4 all-gather.12
  652.3 129.4 all-gather.8
where the time goes:
time: 939 us; the launch traced here: 921 us
  waiting for transfers between devices  400 us (43%)
  other arithmetic  224 us (24%)
  local copies, waits for them, and re-layouts  161 us (17%)
  blocking collectives  92.5 us (10%)
  starting transfers between devices  19.5 us (2%)
  between operations  13.5 us (1%)
    all_gather x4, waiting for transfers between devices, carried_in(): everything = jax.tree.map(lambda part: lax.all_gather(part, axis), value)  371 us
    select_n x128, other arithmetic, turn(): return jax.tree.map(lambda a, b: jnp.where(reached, a, b), new, before)  101 us
    another operation x32, other arithmetic, advance(): summed = jnp.cumsum(terms, axis=0)  71.1 us
    psum x1, blocking collectives, local(): forward_sum, reverse_sum = lax.psum((partials[0], partials[1]), 'grp')  57.8 us
    all_to_all x1, blocking collectives, local(): return lax.all_to_all(gated, 'grp', split_axis=0, concat_axis=1, tiled=True)  34.6 us
    mul x32, local copies, waits for them, and re-layouts, advance(): jnp.exp(rates[None] * centred[:, None, :]) * drive_rows[:, None, :]  30.5 us
    all_to_all x1, waiting for transfers between devices, local(): lax.all_to_all(inner_input, 'grp', split_axis=1, concat_axis=0, tiled=True)  25.7 us
    mul x32, local copies, waits for them, and re-layouts, advance(): return (history[-1], jnp.sum(out_rows[:, :, None] * history, axis=1))  25.2 us
  transfers between devices with their start and end apart: 8, of which 6 were waited for; matrix products, arithmetic and copies ran while one was open for 28% of the time, Pallas kernels for 0%

commit v1 on v0

v1 whole, which is shorter than its diff:
```python
import functools
import math

import jax
import jax.numpy as jnp
from jax import lax
from jax.experimental import pallas as pl
from jax.experimental.pallas import tpu as pltpu
from jax.sharding import PartitionSpec as P

F32 = jnp.float32
BF16 = jnp.bfloat16
LOG2E = math.log2(math.e)
LN2 = math.log(2.0)

CHUNKS = 8
LANES = 128

ROW_CONV = 0
ROW_BIAS = 8
ROW_STEP = 10
ROW_SKIP = 12
ROW_RATE = 16
ROWS_SMALL = 48


def iota(shape, dim):
    return lax.broadcasted_iota(jnp.int32, shape, dim)


def silu(value):
    half = 0.5 * value
    return half + half * jnp.tanh(half)


def softplus(value):
    small = jnp.exp2(jnp.abs(value) * -LOG2E)
    series = small * (1.0 - small * (0.5 - small * (1.0 / 3.0 - small * 0.25)))
    logarithm = LN2 * jnp.log2(1.0 + small)
    return jnp.maximum(value, 0.0) + jnp.where(small < 0.02, series, logarithm)


def dot_t(a, b):
    return lax.dot_general(a, b, (((1,), (1,)), ((), ())), preferred_element_type=F32)


def convolve(tile, x_ref, before_ref, after_ref, small_ref, u_ref, rows_f32):
    rows = x_ref.shape[0]
    steps = rows // CHUNKS
    shard, column = tile // 4, lax.rem(tile, 4)
    cols = pl.ds(pl.multiple_of(tile * LANES, LANES), LANES)
    lanes = pl.ds(pl.multiple_of(column * LANES, LANES), LANES)
    rows_f32[0:16, :] = before_ref[:, cols].astype(F32)
    rows_f32[16 : 16 + rows, :] = x_ref[:, cols].astype(F32)
    rows_f32[16 + rows : 32 + rows, :] = after_ref[:, cols].astype(F32)
    taps = {t: rows_f32[pl.ds(16 + t, CHUNKS, stride=steps), :] for t in range(-3, steps + 3)}
    for branch in range(2):
        weights = [
            jnp.broadcast_to(
                small_ref[shard, ROW_CONV + 4 * branch + j : ROW_CONV + 4 * branch + j + 1, lanes],
                (CHUNKS, LANES),
            )
            for j in range(4)
        ]
        bias = jnp.broadcast_to(
            small_ref[shard, ROW_BIAS + branch : ROW_BIAS + branch + 1, lanes], (CHUNKS, LANES)
        )
        sign = -1 if branch == 0 else 1
        for t in range(0, steps, 2):
            pair = []
            for s in (t, t + 1):
                total = bias
                for j in range(4):
                    total = total + weights[j] * taps[s + sign * (3 - j)]
                pair.append(silu(total))
            u_ref[branch, t * CHUNKS : (t + 2) * CHUNKS, cols] = jnp.concatenate(pair, 0).astype(
                BF16
            )


def spread_maps(branch, maps, in_wide, out_wide, out_half):
    rows = maps.shape[0]
    count = rows * 16
    r, c = iota((count, rows), 0), iota((count, rows), 1)
    pick = ((r >> 7) * CHUNKS + (r & 7) == c).astype(F32).astype(BF16)
    picked = jnp.dot(pick, maps, preferred_element_type=F32)
    r, c = iota((count, 32), 0), iota((count, 32), 1)
    state = (r >> 3) & 15
    ones = jnp.ones((32, LANES), BF16)
    in_wide[branch] = jnp.dot(
        jnp.where(state == c, picked, 0.0).astype(BF16), ones, preferred_element_type=F32
    )
    out_wide[branch] = jnp.dot(
        jnp.where(state + 16 == c, picked, 0.0).astype(BF16), ones, preferred_element_type=F32
    )
    r, c = iota((count, rows), 0), iota((count, rows), 1)
    pick = ((r >> 8) * 16 + (r & 15) == c).astype(F32).astype(BF16)
    picked = jnp.dot(pick, maps, preferred_element_type=F32)
    r, c = iota((count, 32), 0), iota((count, 32), 1)
    state = (r >> 4) & 15
    out_half[branch] = jnp.dot(
        jnp.where(state + 16 == c, picked, 0.0).astype(BF16), ones, preferred_element_type=F32
    ).astype(BF16)


def step_sizes(branch, shard, low, step_weight_ref, small_ref, step_ref):
    width = step_weight_ref.shape[-1]
    rows = low.shape[0]
    for q in range(width // LANES):
        lanes = slice(q * LANES, (q + 1) * LANES)
        value = jnp.dot(low, step_weight_ref[shard, branch, :, lanes], preferred_element_type=F32)
        value = value + small_ref[shard, ROW_STEP + branch : ROW_STEP + branch + 1, lanes]
        step_ref[branch, shard * (width // LANES) + q] = softplus(value).reshape(
            rows // CHUNKS, CHUNKS, LANES
        )


def scan_tile(branch, tile, u_ref, small_ref, step_ref, in_wide, out_wide, y_ref, end_ref):
    steps = step_ref.shape[2]
    shard, column = tile // 4, lax.rem(tile, 4)
    cols = pl.ds(pl.multiple_of(tile * LANES, LANES), LANES)
    lanes = pl.ds(pl.multiple_of(column * LANES, LANES), LANES)
    first = ROW_RATE + 16 * branch
    skip = jnp.broadcast_to(
        small_ref[shard, ROW_SKIP + branch : ROW_SKIP + branch + 1, lanes], (CHUNKS, LANES)
    )
    for start in (0, 8):
        rates = jnp.stack(
            [
                jnp.broadcast_to(
                    small_ref[shard, first + n : first + n + 1, lanes], (CHUNKS, LANES)
                )
                for n in range(start, start + 8)
            ]
        )
        state = jnp.zeros((8, CHUNKS, LANES), F32)
        for j in range(steps):
            t = j if branch == 0 else steps - 1 - j
            size = step_ref[branch, tile, t]
            u = u_ref[branch, pl.ds(t * CHUNKS, CHUNKS), cols].astype(F32)
            at = pl.ds((t * 16 + start) * CHUNKS, 8 * CHUNKS)
            into = in_wide[branch, at, :].reshape(8, CHUNKS, LANES)
            out = out_wide[branch, at, :].reshape(8, CHUNKS, LANES)
            state = jnp.exp2(rates * size[None]) * state + (size * u)[None] * into
            part = jnp.sum(out * state, axis=0)
            if start == 0:
                part = part + skip * u
            if branch == 1 or start > 0:
                part = part + y_ref[tile, t]
            y_ref[tile, t] = part
        end_ref[branch, tile, start * CHUNKS : (start + 8) * CHUNKS, :] = state.reshape(
            8 * CHUNKS, LANES
        )


def chunk_totals(branch, tile, step_ref):
    total = step_ref[branch, tile, 0]
    for t in range(1, step_ref.shape[2]):
        total = total + step_ref[branch, tile, t]
    return total


def device_state(branch, tile, small_ref, step_ref, end_ref, totals, state_ref, elapsed_ref):
    shard, column = tile // 4, lax.rem(tile, 4)
    lanes = pl.ds(pl.multiple_of(column * LANES, LANES), LANES)
    first = ROW_RATE + 16 * branch
    rates = small_ref[shard, first : first + 16, lanes]
    totals[...] = chunk_totals(branch, tile, step_ref)
    state = jnp.zeros((16, LANES), F32)
    elapsed = jnp.zeros((1, LANES), F32)
    for j in range(CHUNKS):
        k = j if branch == 0 else CHUNKS - 1 - j
        span = totals[k : k + 1, :]
        state = jnp.exp2(rates * span) * state + end_ref[branch, tile, pl.ds(k, 16, stride=CHUNKS), :]
        elapsed = elapsed + span
    state_ref[branch, tile] = state
    elapsed_ref[branch, tile] = jnp.broadcast_to(elapsed, (8, LANES))


def front_kernel(
    x_ref, before_ref, after_ref, small_ref, proj_weight_ref, step_weight_ref,
    y_ref, end_ref, step_ref, state_ref, elapsed_ref, out_half,
    u_ref, rows_f32, in_wide, out_wide, totals,
):
    tiles = x_ref.shape[1] // LANES
    shards = small_ref.shape[0]

    def conv_body(tile, _):
        convolve(tile, x_ref, before_ref, after_ref, small_ref, u_ref, rows_f32)
        return 0

    lax.fori_loop(0, tiles, conv_body, 0)
    width = proj_weight_ref.shape[-1]
    for branch in range(2):
        projected = jnp.zeros((x_ref.shape[0], proj_weight_ref.shape[2]), F32)
        for shard in range(shards):
            projected = projected + dot_t(
                u_ref[branch, :, shard * width : (shard + 1) * width], proj_weight_ref[shard, branch]
            )
        projected = projected.astype(BF16)
        spread_maps(branch, projected[:, 128:160], in_wide, out_wide, out_half)
        low = projected[:, 0:128]

        def step_body(shard, _):
            step_sizes(branch, shard, low, step_weight_ref, small_ref, step_ref)
            return 0

        lax.fori_loop(0, shards, step_body, 0)

        def scan_body(tile, _):
            scan_tile(
                branch, tile, u_ref, small_ref, step_ref, in_wide, out_wide, y_ref, end_ref
            )
            return 0

        lax.fori_loop(0, tiles, scan_body, 0)

        def state_body(tile, _):
            device_state(
                branch, tile, small_ref, step_ref, end_ref, totals, state_ref, elapsed_ref
            )
            return 0

        lax.fori_loop(0, tiles, state_body, 0)


def correct_tile(
    branch, tile, small_ref, step_ref, end_ref, out_half, carry_ref, y_ref, totals, chunk_carry
):
    shard, column = tile // 4, lax.rem(tile, 4)
    lanes = pl.ds(pl.multiple_of(column * LANES, LANES), LANES)
    first = ROW_RATE + 16 * branch
    steps = step_ref.shape[2]
    rates = small_ref[shard, first : first + 16, lanes]
    totals[...] = chunk_totals(branch, tile, step_ref)
    carry = carry_ref[branch, tile]
    for j in range(CHUNKS):
        k = j if branch == 0 else CHUNKS - 1 - j
        chunk_carry[pl.ds(k, 16, stride=CHUNKS), :] = carry
        if j < CHUNKS - 1:
            carry = (
                jnp.exp2(rates * totals[k : k + 1, :]) * carry
                + end_ref[branch, tile, pl.ds(k, 16, stride=CHUNKS), :]
            )
    entering = []
    wide = []
    for n in range(16):
        one = chunk_carry[n * CHUNKS : (n + 1) * CHUNKS, :]
        entering.append(jnp.concatenate([one, one], 0).astype(BF16))
        rate = small_ref[shard, first + n : first + n + 1, lanes]
        wide.append(jnp.broadcast_to(rate, (16, LANES)).astype(BF16))
    elapsed = jnp.zeros((CHUNKS, LANES), F32)
    for j in range(0, steps, 2):
        pair = []
        for i in (j, j + 1):
            t = i if branch == 0 else steps - 1 - i
            elapsed = elapsed + step_ref[branch, tile, t]
            pair.append(elapsed)
        low = j if branch == 0 else steps - 2 - j
        if branch == 1:
            pair = pair[::-1]
        spans = jnp.concatenate(pair, 0).astype(BF16)
        total = None
        for n in range(16):
            at = (low // 2 * 16 + n) * 16
            part = jnp.exp2(wide[n] * spans) * entering[n] * out_half[branch, at : at + 16, :]
            total = part if total is None else total + part
        total = total.astype(F32)
        y_ref[tile, low] = y_ref[tile, low] + total[:CHUNKS]
        y_ref[tile, low + 1] = y_ref[tile, low + 1] + total[CHUNKS:]


def gate_tile(tile, y_ref, gate_ref, result_ref, rows_f32):
    steps = y_ref.shape[1]
    rows = gate_ref.shape[0]
    cols = pl.ds(pl.multiple_of(tile * LANES, LANES), LANES)
    for t in range(steps):
        rows_f32[pl.ds(t, CHUNKS, stride=steps), :] = y_ref[tile, t]
    mixed = rows_f32[0:rows, :].astype(BF16).astype(F32)
    result_ref[:, cols] = (mixed * silu(gate_ref[:, cols].astype(F32))).astype(BF16)


def back_kernel(
    y_in_ref, end_ref, step_ref, out_half, small_ref, carry_ref, gate_ref, result_ref,
    y_ref, rows_f32, totals, chunk_carry,
):
    tiles = y_in_ref.shape[0]

    def body(tile, _):
        y_ref[tile] = y_in_ref[tile]
        for branch in range(2):
            correct_tile(
                branch, tile, small_ref, step_ref, end_ref, out_half, carry_ref, y_ref, totals,
                chunk_carry,
            )
        gate_tile(tile, y_ref, gate_ref, result_ref, rows_f32)
        return 0

    lax.fori_loop(0, tiles, body, 0)


VMEM = pl.BlockSpec(memory_space=pltpu.VMEM)


def run_front(x, before, after, small, proj_weight, step_weight):
    rows, channels = x.shape
    tiles, steps = channels // LANES, rows // CHUNKS
    shape = jax.ShapeDtypeStruct
    return pl.pallas_call(
        front_kernel,
        out_shape=(
            shape((tiles, steps, CHUNKS, LANES), F32),
            shape((2, tiles, 16 * CHUNKS, LANES), F32),
            shape((2, tiles, steps, CHUNKS, LANES), F32),
            shape((2, tiles, 16, LANES), F32),
            shape((2, tiles, 8, LANES), F32),
            shape((2, rows * 16, LANES), BF16),
        ),
        in_specs=[VMEM] * 6,
        out_specs=(VMEM,) * 6,
        scratch_shapes=[
            pltpu.VMEM((2, rows, channels), BF16),
            pltpu.VMEM((rows + 32, LANES), F32),
            pltpu.VMEM((2, rows * 16, LANES), F32),
            pltpu.VMEM((2, rows * 16, LANES), F32),
            pltpu.VMEM((CHUNKS, LANES), F32),
        ],
        compiler_params=pltpu.CompilerParams(vmem_limit_bytes=56 << 20),
    )(x, before, after, small, proj_weight, step_weight)


def run_back(y, end, step, out_half, small, carry, gate):
    rows, channels = gate.shape
    return pl.pallas_call(
        back_kernel,
        out_shape=jax.ShapeDtypeStruct((rows, channels), BF16),
        in_specs=[VMEM] * 7,
        out_specs=VMEM,
        scratch_shapes=[
            pltpu.VMEM(y.shape, F32),
            pltpu.VMEM((rows + 32, LANES), F32),
            pltpu.VMEM((CHUNKS, LANES), F32),
            pltpu.VMEM((16 * CHUNKS, LANES), F32),
        ],
        compiler_params=pltpu.CompilerParams(vmem_limit_bytes=56 << 20),
    )(y, end, step, out_half, small, carry, gate)


def entering_states(state, elapsed, decay_rate):
    tiles = state.shape[1]
    grp = lax.axis_size("grp")
    seq = lax.axis_size("seq")
    width = tiles // grp
    here_g, here_s = lax.axis_index("grp"), lax.axis_index("seq")
    states = state.reshape(2, grp, width, 16, LANES).transpose(1, 0, 2, 3, 4)
    spans = elapsed.reshape(2, grp, width, 1, LANES).transpose(1, 0, 2, 3, 4)
    both = jnp.concatenate([states, spans], 3)
    both = lax.all_to_all(both, "grp", split_axis=0, concat_axis=0, tiled=True)
    rates = decay_rate.reshape(2, 16, width, LANES).transpose(0, 2, 1, 3)

    def through(carry, part, branch):
        return jnp.exp(-rates[branch] * part[branch, :, 16:]) * carry + part[branch, :, :16]

    totals = []
    for branch in range(2):
        order = range(grp) if branch == 0 else range(grp - 1, -1, -1)
        carry = jnp.zeros((width, 16, LANES), F32)
        for g in order:
            carry = through(carry, both[g], branch)
        span = jnp.sum(both[:, branch, :, 16:], axis=0)
        totals.append(jnp.concatenate([carry, span], 1))
    everything = lax.all_gather(jnp.stack(totals), "seq")
    carries = []
    for branch in range(2):
        carry = jnp.zeros((width, 16, LANES), F32)

        def turn(i, carry, branch=branch):
            at = i if branch == 0 else seq - 1 - i
            reached = at < here_s if branch == 0 else at > here_s
            return jnp.where(reached, through(carry, everything[at], branch), carry)

        carry = lax.fori_loop(0, seq, turn, carry)
        order = range(grp) if branch == 0 else range(grp - 1, -1, -1)
        each = [None] * grp
        for g in order:
            each[g] = carry
            carry = through(carry, both[g], branch)
        carries.append(jnp.stack(each))
    back = jnp.stack(carries, 1)
    back = lax.all_to_all(back, "grp", split_axis=0, concat_axis=0, tiled=True)
    return back.transpose(1, 0, 2, 3, 4).reshape(2, tiles, 16, LANES)


def local(
    inner_input,
    inner_gate,
    conv_weight,
    conv_bias,
    proj_weight,
    step_weight,
    step_bias,
    decay_rate,
    skip_gain,
):
    width = conv_weight.shape[2]
    small = jnp.concatenate(
        [
            conv_weight.reshape(8, width),
            conv_bias,
            step_bias,
            skip_gain,
            jnp.zeros((2, width), F32),
            decay_rate.reshape(32, width) * -LOG2E,
        ],
        0,
    )
    small = lax.all_gather(small, "grp")
    proj_weight = lax.all_gather(jnp.swapaxes(proj_weight, 1, 2), "grp")
    step_weight = lax.all_gather(step_weight, "grp")
    axes = ("seq", "grp")
    count = lax.axis_size("seq") * lax.axis_size("grp")
    before = lax.ppermute(inner_input[-16:], axes, [(i, i + 1) for i in range(count - 1)])
    after = lax.ppermute(inner_input[:16], axes, [(i + 1, i) for i in range(count - 1)])
    y, end, step, state, elapsed, out_half = run_front(
        inner_input, before, after, small, proj_weight, step_weight
    )
    carry = entering_states(state, elapsed[:, :, 0], decay_rate)
    return run_back(y, end, step, out_half, small, carry, inner_gate)


def solution(mesh):
    placed = (
        P(("seq", "grp"), None),
        P(("seq", "grp"), None),
        P(None, None, "grp"),
        P(None, "grp"),
        P(None, "grp", None),
        P(None, None, "grp"),
        P(None, "grp"),
        P(None, None, "grp"),
        P(None, "grp"),
    )
    return jax.shard_map(
        local, mesh=mesh, in_specs=placed, out_specs=P(("seq", "grp"), None), check_vma=False
    )
```

time: 939 us -> 503 us (0.54); the launches traced: 921 us -> 499 us
  other arithmetic: 224 us -> 5.51 us
  waiting for transfers between devices: 400 us -> 231 us
  Pallas kernels: 0 us -> 58.6 us
  blocking collectives: 92.5 us -> 42 us
  local copies, waits for them, and re-layouts: 161 us -> 128 us
    all_gather x4 -> x3, waiting for transfers between devices: 371 us -> 215 us  [the longest x1 150 us: entering_states(): everything = lax.all_gather(jnp.stack(totals), 'seq')]
    select_n x128, other arithmetic: 101 us -> 2.22 us  [turn(): return jnp.where(reached, through(carry, everything[at], branch), carry)]
    squeeze x32 -> x129, local copies, waits for them, and re-layouts: 19.4 us -> 116 us  [the longest x128 116 us: turn(): return jnp.where(reached, through(carry, everything[at], branch), carry)]
    another operation x70 -> x5, other arithmetic: 80.3 us -> 0.86 us  [the longest x3 0.67 us: entering_states(): everything = lax.all_gather(jnp.stack(totals), 'seq')]
    pallas_call x0 -> x2, Pallas kernels: none -> 58.6 us  [the longest x1 40.8 us: run_front(): pl.pallas_call(front_kernel, out_shape=(shape((tiles, steps, CHUNKS, LANE...]
    psum x1 -> x0, blocking collectives: 57.8 us -> none  [local(): forward_sum, reverse_sum = lax.psum((partials[0], partials[1]), 'grp')]
    mul x64 -> x4, local copies, waits for them, and re-layouts: 55.7 us -> 0.02 us  [through(): -rates[branch] * part[branch, :, 16:]]
    rev x5 -> x0, local copies, waits for them, and re-layouts: 43.9 us -> none  [the longest x1 15.5 us: local(): activation = jnp.flip(activation, 0)]
  transfers between devices with their start and end apart: 8 -> 6, of which waited for: 6 -> 4; matrix products, arithmetic and copies ran while one was open for 28% -> 1% of each run, Pallas kernels for 0% -> 0%
where the time goes in v1:
time: 503 us; the launch traced here: 499 us
  waiting for transfers between devices  231 us (46%)
  local copies, waits for them, and re-layouts  128 us (25%)
  Pallas kernels  58.6 us (12%)
  blocking collectives  42 us (8%)
  starting transfers between devices  15.9 us (3%)
  between operations  13.3 us (3%)
  other arithmetic  5.51 us (1%)
    all_gather x1, waiting for transfers between devices, entering_states(): everything = lax.all_gather(jnp.stack(totals), 'seq')  150 us
    squeeze x128, local copies, waits for them, and re-layouts, turn(): return jnp.where(reached, through(carry, everything[at], branch), carry)  116 us
    all_gather x1, waiting for transfers between devices, local(): proj_weight = lax.all_gather(jnp.swapaxes(proj_weight, 1, 2), 'grp')  46.4 us
    pallas_call x1, Pallas kernels, run_front(): pl.pallas_call(front_kernel, out_shape=(shape((tiles, steps, CHUNKS, LANE...  40.8 us
    all_to_all x1, blocking collectives, entering_states(): back = lax.all_to_all(back, 'grp', split_axis=0, concat_axis=0, tiled=True)  24.3 us
    pallas_call x1, Pallas kernels, run_back(): pl.pallas_call(back_kernel, out_shape=jax.ShapeDtypeStruct((rows, channel...  17.9 us
    all_gather x1, waiting for transfers between devices, local(): step_weight = lax.all_gather(step_weight, 'grp')  17.8 us
    all_gather x1, blocking collectives, local(): small = lax.all_gather(small, 'grp')  17.7 us
  transfers between devices with their start and end apart: 6, of which 4 were waited for; matrix products, arithmetic and copies ran while one was open for 1% of the time, Pallas kernels for 0%

profile of v1, /device:TPU:1, one launch (start us, length us, event | category | flops | bytes accessed | tf_op | source)
XLA Modules:
  0.0 498.9 jit_solution(1034230387869034188)
XLA Ops:
  8.0 1.0 fusion.8
  9.0 4.6 collective-permute-start
  13.6 5.5 %collective-permute-start.1 = (bf16[16,4096]{1,0:T(8,128)(2,1)S(1)}, bf16[16,4096]{1,0:T(8,128)(2,1)S(1)}, u32[]{:S(2)}, u32[]{:S(2)}) collective-permute-start(bf16[16,4096]{1,0:T(8,128)(2,1)S(1)} %get-tuple-element.369), channel_id=1, source_target_pairs={{1,0},{2,1},{3,2},{4,3},{5,4},{6,5},{7,6},{8,7},{9,8},{10,9},{11,1... | collective-permute-start | bytes 393224 | tf_op jit(solution)/shard_map/ppermute | solution.py:423
  21.4 17.7 %all-gather = f32[384,512]{1,0:T(8,128)} all-gather(f32[48,512]{1,0:T(8,128)S(1)} %concatenate.12), channel_id=2, replica_groups=mesh['seq'=64,'grp'=8] {'grp'}, dimensions={0}, use_global_device_ids=true | all-gather | bytes 884736 | tf_op jit(solution)/shard_map/all_gather | solution.py:417
  39.1 17.8 %all-gather.10.cloned.1.call-done = bf16[16,128,512]{2,1,0:T(8,128)(2,1)} async-done(((bf16[2,128,512]{2,1,0:T(8,128)(2,1)}), bf16[16,128,512]{2,1,0:T(8,128)(2,1)}) %all-gather.10.cloned.1.call-update) | async-done | bytes 2097168 | tf_op jit(solution)/shard_map/all_gather | solution.py:419
  57.0 46.4 %all-gather.8.cloned.1.call-done = bf16[16,160,512]{2,1,0:T(8,128)(2,1)} async-done(((bf16[2,160,512]{2,1,0:T(8,128)(2,1)}), bf16[16,160,512]{2,1,0:T(8,128)(2,1)}) %all-gather.8.cloned.1.call-update) | async-done | bytes 2621456 | tf_op jit(solution)/shard_map/all_gather | solution.py:418
  103.4 40.8 %shard_map.91 = (f32[32,16,8,128]{3,2,1,0:T(8,128)}, f32[2,32,128,128]{3,2,1,0:T(8,128)}, f32[2,32,16,8,128]{4,3,2,1,0:T(8,128)}, f32[2,32,16,128]{3,2,1,0:T(8,1...) custom-call(bf16[128,4096]{1,0:T(8,128)(2,1)} %x_ref.1, bf16[16,4096]{1,0:T(8,128)(2,1)} %copy-done.1, ...), custom_call_target="tpu_custom_call" | custom-call | tf_op jit(solution)/shard_map/pallas_call | solution.py:309
  144.1 1.2 copy.43
  145.4 1.0 slice.274
  146.4 0.9 pad_maximum_fusion
  147.3 5.8 %all-to-all-start = ((f32[8,2,4,17,128]{4,2,3,1,0:T(4,128)}), f32[8,2,4,17,128]{4,2,3,1,0:T(4,128)S(1)}, u32[]{:S(2)}, u32[]{:S(2)}) async-start(f32[8,2,4,17,128]{4,2,3,1,0:T(4,128)} %pad_maximum_fusion), calls=%async_computation | async-start | bytes 1114112 | tf_op jit(solution)/shard_map/all_to_all | solution.py:358
  153.1 15.2 %all-to-all-done = f32[8,2,4,17,128]{4,2,3,1,0:T(4,128)S(1)} async-done(((f32[8,2,4,17,128]{4,2,3,1,0:T(4,128)}), f32[8,2,4,17,128]{4,2,3,1,0:T(4,128)S(1)}, u32[]{:S(2)}, u32[]{:S(2)}) %all-to-all-start) | async-done | bytes 557088 | tf_op jit(solution)/shard_map/all_to_all | solution.py:358
  169.4 150.4 %all-gather.12.cloned.1.call-done = f32[128,4,17,128]{3,1,2,0:T(4,128)} async-done(((f32[2,4,17,128]{3,1,2,0:T(4,128)}), f32[128,4,17,128]{3,1,2,0:T(4,128)}) %all-gather.12.cloned.1.call-update) | async-done | bytes 4456464 | tf_op jit(solution)/shard_map/all_gather | solution.py:372
  319.8 5.7 %copy.25 = f32[64,2,4,17,128]{4,3,2,1,0:T(8,128)} copy(f32[64,2,4,17,128]{4,2,3,1,0:T(4,128)} %bitcast.316) | data formatting | bytes 8912896
  325.5 61.2 %while.32 = (s32[]{:T(128)}, f32[4,16,128]{2,1,0:T(8,128)S(1)}, s32[]{:T(128)}, f32[64,2,4,17,128]{4,3,2,1,0:T(8,128)}, f32[4,16,128]{2,1,0:T(8,128)S(1)}, /*index=5*/s32[]{:T(128)}, s32[]{:T(128)}) while((s32[]{:T(128)}, f32[4,16,128]{2,1,0:T(8,128)S(1)}, s32[]{:T(128)}, f32[64,2,4,17,128]{4,3,2,1,0:T(8,128)}, ...), condition=%wide.region_3.4_spmd.clone, body=%wide.region_2.3_spmd.clone.sunk | while | flops 40964 | bytes 276581 | solution.py:382
  386.9 61.9 %while.33 = (s32[]{:T(128)}, f32[4,16,128]{2,1,0:T(8,128)S(1)}, s32[]{:T(128)}, f32[64,2,4,17,128]{4,3,2,1,0:T(8,128)}, f32[4,16,128]{2,1,0:T(8,128)S(1)}, /*index=5*/s32[]{:T(128)}, s32[]{:T(128)}, s32[]{:T(128)}, s32[]{:T(128)}) while((s32[]{:T(128)}, f32[4,16,128]{2,1,0:T(8,128)S(1)}, s32[]{:T(128)}, ...), condition=%wide.region_5.6_spmd.clone, body=%wide.region_4.5_spmd.clone.sunk | while | flops 40968 | bytes 276643 | solution.py:382
  386.9 0.9 dynamic-slice_bitcast_fusion.5
  387.9 0.9 dynamic-slice_bitcast_fusion.5
  388.8 0.9 dynamic-slice_bitcast_fusion.5
  389.8 0.9 dynamic-slice_bitcast_fusion.5
  390.8 0.9 dynamic-slice_bitcast_fusion.5
  391.7 0.9 dynamic-slice_bitcast_fusion.5
  392.7 0.9 dynamic-slice_bitcast_fusion.5
  394.6 0.9 dynamic-slice_bitcast_fusion.5
  395.6 0.9 dynamic-slice_bitcast_fusion.5
  396.6 0.9 dynamic-slice_bitcast_fusion.5
  397.5 0.9 dynamic-slice_bitcast_fusion.5
  398.5 0.9 dynamic-slice_bitcast_fusion.5
  399.5 0.9 dynamic-slice_bitcast_fusion.5
  400.4 0.9 dynamic-slice_bitcast_fusion.5
  401.4 0.9 dynamic-slice_bitcast_fusion.5
  404.3 0.9 dynamic-slice_bitcast_fusion.5
  405.3 0.9 dynamic-slice_bitcast_fusion.5
  406.2 0.9 dynamic-slice_bitcast_fusion.5
  407.2 0.9 dynamic-slice_bitcast_fusion.5
  408.2 0.9 dynamic-slice_bitcast_fusion.5
  409.1 0.9 dynamic-slice_bitcast_fusion.5
  410.1 0.9 dynamic-slice_bitcast_fusion.5
  411.1 0.9 dynamic-slice_bitcast_fusion.5
  413.0 0.9 dynamic-slice_bitcast_fusion.5
  414.0 0.9 dynamic-slice_bitcast_fusion.5
  414.9 0.9 dynamic-slice_bitcast_fusion.5
  415.9 0.9 dynamic-slice_bitcast_fusion.5
  416.9 0.9 dynamic-slice_bitcast_fusion.5
  417.8 0.9 dynamic-slice_bitcast_fusion.5
  418.8 0.9 dynamic-slice_bitcast_fusion.5
  449.4 24.3 %all_to_all.10 = f32[8,2,4,16,128]{4,2,3,1,0:T(4,128)S(1)} all-to-all(f32[8,2,4,16,128]{4,2,3,1,0:T(4,128)S(1)} %copy.33), channel_id=1, replica_groups=mesh['seq'=64,'grp'=8] {'grp'}, dimensions={0} | all-to-all | bytes 1048576 | tf_op jit(solution)/shard_map/all_to_all | solution.py:390
  474.5 17.9 %shard_map.92 = bf16[128,4096]{1,0:T(8,128)(2,1)} custom-call(f32[32,16,8,128]{3,2,1,0:T(8,128)} %get-tuple-element.273.y_in_ref, f32[2,32,128,128]{3,2,1,0:T(8,128)} %get-tuple-element.274.end_ref, f32[2,32,16,8,128]{4,3,2,1,0:T(8,128)} %get-tuple-element.275.step_ref, bf16[2,2048,128]{2,1,0:T(8,128)(2,1)} %get-tuple-element.276.out_half, ...), custom_call_target="tpu_custom_call" | custom-call | tf_op jit(solution)/shard_map/pallas_call | solution.py:334
  (406 shorter events, 97.8 us)
Async XLA Ops:
  6.5 50.4 %all-gather.10.cloned.1.call-start = ((), (), s32[]{:S(2)}) async-start(), calls=%async_computation.3 | async-start | bytes 2359296 | tf_op jit(solution)/shard_map/all_gather | solution.py:419
  7.3 96.1 %all-gather.8.cloned.1.call-start = ((), (), s32[]{:S(2)}) async-start(), calls=%async_computation.2 | async-start | bytes 2949120 | tf_op jit(solution)/shard_map/all_gather | solution.py:418
  9.0 30.1 %collective-permute-start = (bf16[16,4096]{1,0:T(8,128)(2,1)S(1)}, bf16[16,4096]{1,0:T(8,128)(2,1)S(1)}, u32[]{:S(2)}, u32[]{:S(2)}) collective-permute-start(bf16[16,4096]{1,0:T(8,128)(2,1)S(1)} %get-tuple-element.370), channel_id=1, source_target_pairs={{0,1},{1,2},{2,3},{3,4},{4,5},{5,6},{6,7},{7,8},{8,9},{9,10},{10,1... | collective-permute-start | bytes 393224 | tf_op jit(solution)/shard_map/ppermute | solution.py:422
  13.6 25.5 %collective-permute-start.1 = (bf16[16,4096]{1,0:T(8,128)(2,1)S(1)}, bf16[16,4096]{1,0:T(8,128)(2,1)S(1)}, u32[]{:S(2)}, u32[]{:S(2)}) collective-permute-start(bf16[16,4096]{1,0:T(8,128)(2,1)S(1)} %get-tuple-element.369), channel_id=1, source_target_pairs={{1,0},{2,1},{3,2},{4,3},{5,4},{6,5},{7,6},{8,7},{9,8},{10,9},{11,1... | collective-permute-start | bytes 393224 | tf_op jit(solution)/shard_map/ppermute | solution.py:423
  39.1 64.2 %copy-start.1 = (bf16[16,4096]{1,0:T(8,128)(2,1)}, bf16[16,4096]{1,0:T(8,128)(2,1)S(1)}, u32[]{:S(2)}) copy-start(bf16[16,4096]{1,0:T(8,128)(2,1)S(1)} %collective-permute-done.before_ref) | copy-start | bytes 393220
  39.1 64.2 %copy-start.2 = (bf16[16,4096]{1,0:T(8,128)(2,1)}, bf16[16,4096]{1,0:T(8,128)(2,1)S(1)}, u32[]{:S(2)}) copy-start(bf16[16,4096]{1,0:T(8,128)(2,1)S(1)} %collective-permute-done.1.after_ref) | copy-start | bytes 393220
  103.4 49.7 %copy-start = (f32[2,16,512]{2,1,0:T(8,128)S(1)}, f32[2,16,512]{2,1,0:T(8,128)}, u32[]{:S(2)}) copy-start(f32[2,16,512]{2,1,0:T(8,128)} %param.20) | copy-start | bytes 196612
  147.3 21.0 %all-to-all-start = ((f32[8,2,4,17,128]{4,2,3,1,0:T(4,128)}), f32[8,2,4,17,128]{4,2,3,1,0:T(4,128)S(1)}, u32[]{:S(2)}, u32[]{:S(2)}) async-start(f32[8,2,4,17,128]{4,2,3,1,0:T(4,128)} %pad_maximum_fusion), calls=%async_computation | async-start | bytes 1114112 | tf_op jit(solution)/shard_map/all_to_all | solution.py:358
  153.1 166.7 %all-gather.12.cloned.1.call-start = ((), (), s32[]{:S(2)}) async-start(), calls=%async_computation.4 | async-start | bytes 4526080 | tf_op jit(solution)/shard_map/all_gather | solution.py:372
Sparse Core Ops, SparseCore 0:
  9.4 47.4 all-gather.9
  59.0 44.2 all-gather.7
  169.5 150.3 all-gather.11

commit v2 on v1

v2 whole, which is shorter than its diff:
```python
import functools
import math

import jax
import jax.numpy as jnp
from jax import lax
from jax.experimental import pallas as pl
from jax.experimental.pallas import tpu as pltpu
from jax.sharding import PartitionSpec as P

F32 = jnp.float32
BF16 = jnp.bfloat16
LOG2E = math.log2(math.e)
LN2 = math.log(2.0)

CHUNKS = 8
LANES = 128

ROW_CONV = 0
ROW_BIAS = 8
ROW_STEP = 10
ROW_SKIP = 12
ROW_RATE = 16
ROWS_SMALL = 48
HALO = 16
MESH = pl.DeviceIdType.MESH


def iota(shape, dim):
    return lax.broadcasted_iota(jnp.int32, shape, dim)


def silu(value):
    half = 0.5 * value
    return half + half * jnp.tanh(half)


def softplus(value):
    small = jnp.exp2(jnp.abs(value) * -LOG2E)
    series = small * (1.0 - small * (0.5 - small * (1.0 / 3.0 - small * 0.25)))
    logarithm = LN2 * jnp.log2(1.0 + small)
    return jnp.maximum(value, 0.0) + jnp.where(small < 0.02, series, logarithm)


def dot_t(a, b):
    return lax.dot_general(a, b, (((1,), (1,)), ((), ())), preferred_element_type=F32)


def convolve(tile, rows_ref, first, last, small_ref, u_ref, rows_f32):
    rows = rows_ref.shape[0] - 2 * HALO
    steps = rows // CHUNKS
    shard, column = lax.div(tile, 4), lax.rem(tile, 4)
    cols = pl.ds(pl.multiple_of(tile * LANES, LANES), LANES)
    lanes = pl.ds(pl.multiple_of(column * LANES, LANES), LANES)
    rows_f32[0:HALO, :] = rows_ref[0:HALO, cols].astype(F32) * first
    rows_f32[HALO : HALO + rows, :] = rows_ref[HALO : HALO + rows, cols].astype(F32)
    rows_f32[HALO + rows : 2 * HALO + rows, :] = (
        rows_ref[HALO + rows : 2 * HALO + rows, cols].astype(F32) * last
    )
    taps = {t: rows_f32[pl.ds(HALO + t, CHUNKS, stride=steps), :] for t in range(-3, steps + 3)}
    for branch in range(2):
        weights = [
            jnp.broadcast_to(
                small_ref[shard, ROW_CONV + 4 * branch + j : ROW_CONV + 4 * branch + j + 1, lanes],
                (CHUNKS, LANES),
            )
            for j in range(4)
        ]
        bias = jnp.broadcast_to(
            small_ref[shard, ROW_BIAS + branch : ROW_BIAS + branch + 1, lanes], (CHUNKS, LANES)
        )
        sign = -1 if branch == 0 else 1
        for t in range(0, steps, 2):
            pair = []
            for s in (t, t + 1):
                total = bias
                for j in range(4):
                    total = total + weights[j] * taps[s + sign * (3 - j)]
                pair.append(silu(total))
            u_ref[branch, t * CHUNKS : (t + 2) * CHUNKS, cols] = jnp.concatenate(pair, 0).astype(
                BF16
            )


def spread_maps(branch, maps, in_wide, out_wide, out_half):
    rows = maps.shape[0]
    count = rows * 16
    r, c = iota((count, rows), 0), iota((count, rows), 1)
    pick = ((r >> 7) * CHUNKS + (r & 7) == c).astype(F32).astype(BF16)
    picked = jnp.dot(pick, maps, preferred_element_type=F32)
    r, c = iota((count, 32), 0), iota((count, 32), 1)
    state = (r >> 3) & 15
    ones = jnp.ones((32, LANES), BF16)
    in_wide[branch] = jnp.dot(
        jnp.where(state == c, picked, 0.0).astype(BF16), ones, preferred_element_type=F32
    )
    out_wide[branch] = jnp.dot(
        jnp.where(state + 16 == c, picked, 0.0).astype(BF16), ones, preferred_element_type=F32
    )
    r, c = iota((count, rows), 0), iota((count, rows), 1)
    pick = ((r >> 8) * 16 + (r & 15) == c).astype(F32).astype(BF16)
    picked = jnp.dot(pick, maps, preferred_element_type=F32)
    r, c = iota((count, 32), 0), iota((count, 32), 1)
    state = (r >> 4) & 15
    out_half[branch] = jnp.dot(
        jnp.where(state + 16 == c, picked, 0.0).astype(BF16), ones, preferred_element_type=F32
    ).astype(BF16)


def step_sizes(branch, shard, low, step_weight_ref, small_ref, step_ref):
    width = step_weight_ref.shape[-1]
    rows = low.shape[0]
    for q in range(width // LANES):
        lanes = slice(q * LANES, (q + 1) * LANES)
        value = jnp.dot(low, step_weight_ref[shard, branch, :, lanes], preferred_element_type=F32)
        value = value + small_ref[shard, ROW_STEP + branch : ROW_STEP + branch + 1, lanes]
        step_ref[branch, shard * (width // LANES) + q] = softplus(value).reshape(
            rows // CHUNKS, CHUNKS, LANES
        )


def scan_tile(
    branch, tile, u_ref, small_ref, step_ref, in_wide, out_wide, y_ref, end_ref, total_ref, fresh
):
    steps = step_ref.shape[2]
    shard, column = lax.div(tile, 4), lax.rem(tile, 4)
    cols = pl.ds(pl.multiple_of(tile * LANES, LANES), LANES)
    lanes = pl.ds(pl.multiple_of(column * LANES, LANES), LANES)
    first = ROW_RATE + 16 * branch
    skip = jnp.broadcast_to(
        small_ref[shard, ROW_SKIP + branch : ROW_SKIP + branch + 1, lanes], (CHUNKS, LANES)
    )
    for start in (0, 8):
        rates = jnp.stack(
            [
                jnp.broadcast_to(
                    small_ref[shard, first + n : first + n + 1, lanes], (CHUNKS, LANES)
                )
                for n in range(start, start + 8)
            ]
        )
        state = jnp.zeros((8, CHUNKS, LANES), F32)
        elapsed = jnp.zeros((CHUNKS, LANES), F32)
        for j in range(steps):
            t = j if branch == 0 else steps - 1 - j
            size = step_ref[branch, tile, t]
            u = u_ref[branch, pl.ds(t * CHUNKS, CHUNKS), cols].astype(F32)
            at = pl.ds((t * 16 + start) * CHUNKS, 8 * CHUNKS)
            into = in_wide[branch, at, :].reshape(8, CHUNKS, LANES)
            out = out_wide[branch, at, :].reshape(8, CHUNKS, LANES)
            state = jnp.exp2(rates * size[None]) * state + (size * u)[None] * into
            part = jnp.sum(out * state, axis=0)
            if start == 0:
                part = part + skip * u
                elapsed = elapsed + size
            if start > 0 or not fresh:
                part = part + y_ref[tile, t]
            y_ref[tile, t] = part
        if start == 0:
            total_ref[branch, tile] = elapsed
        end_ref[branch, tile, start * CHUNKS : (start + 8) * CHUNKS, :] = state.reshape(
            8 * CHUNKS, LANES
        )


def device_state(branch, tile, small_ref, end_ref, total_ref, message_ref):
    shard, column = lax.div(tile, 4), lax.rem(tile, 4)
    lanes = pl.ds(pl.multiple_of(column * LANES, LANES), LANES)
    first = ROW_RATE + 16 * branch
    rates = small_ref[shard, first : first + 16, lanes]
    state = jnp.zeros((16, LANES), F32)
    elapsed = jnp.zeros((1, LANES), F32)
    for j in range(CHUNKS):
        k = j if branch == 0 else CHUNKS - 1 - j
        span = total_ref[branch, tile, k : k + 1, :]
        state = jnp.exp2(rates * span) * state + end_ref[branch, tile, pl.ds(k, 16, stride=CHUNKS), :]
        elapsed = elapsed + span
    message_ref[branch, tile] = as_message(state, elapsed)


def as_message(state, elapsed):
    high = elapsed.astype(BF16).astype(F32)
    low = elapsed - high
    row = iota((16, LANES), 0)
    times = jnp.where(row == 0, high, jnp.where(row == 1, low, 0.0))
    return jnp.concatenate([state, times], 0).astype(BF16)


def of_message(message):
    values = message.astype(F32)
    return values[0:16], values[16:17] + values[17:18]


def correct_tile(
    branch, tile, small_ref, step_ref, end_ref, out_half, carry_ref, y_ref, total_ref, chunk_carry
):
    shard, column = lax.div(tile, 4), lax.rem(tile, 4)
    lanes = pl.ds(pl.multiple_of(column * LANES, LANES), LANES)
    first = ROW_RATE + 16 * branch
    steps = step_ref.shape[2]
    rates = small_ref[shard, first : first + 16, lanes]
    carry = carry_ref[branch, tile].astype(F32)
    for j in range(CHUNKS):
        k = j if branch == 0 else CHUNKS - 1 - j
        chunk_carry[pl.ds(k, 16, stride=CHUNKS), :] = carry
        if j < CHUNKS - 1:
            carry = (
                jnp.exp2(rates * total_ref[branch, tile, k : k + 1, :]) * carry
                + end_ref[branch, tile, pl.ds(k, 16, stride=CHUNKS), :]
            )
    entering = []
    wide = []
    for n in range(16):
        one = chunk_carry[n * CHUNKS : (n + 1) * CHUNKS, :]
        entering.append(jnp.concatenate([one, one], 0).astype(BF16))
        rate = small_ref[shard, first + n : first + n + 1, lanes]
        wide.append(jnp.broadcast_to(rate, (16, LANES)).astype(BF16))
    elapsed = jnp.zeros((CHUNKS, LANES), F32)
    for j in range(0, steps, 2):
        pair = []
        for i in (j, j + 1):
            t = i if branch == 0 else steps - 1 - i
            elapsed = elapsed + step_ref[branch, tile, t]
            pair.append(elapsed)
        low = j if branch == 0 else steps - 2 - j
        if branch == 1:
            pair = pair[::-1]
        spans = jnp.concatenate(pair, 0).astype(BF16)
        total = None
        for n in range(16):
            at = ((low // 2) * 16 + n) * 16
            part = jnp.exp2(wide[n] * spans) * entering[n] * out_half[branch, at : at + 16, :]
            total = part if total is None else total + part
        total = total.astype(F32)
        y_ref[tile, low] = y_ref[tile, low] + total[:CHUNKS]
        y_ref[tile, low + 1] = y_ref[tile, low + 1] + total[CHUNKS:]


def gate_tile(tile, y_ref, gate_ref, result_ref, rows_f32):
    steps = y_ref.shape[1]
    rows = gate_ref.shape[0]
    cols = pl.ds(pl.multiple_of(tile * LANES, LANES), LANES)
    for t in range(steps):
        rows_f32[pl.ds(t, CHUNKS, stride=steps), :] = y_ref[tile, t]
    mixed = rows_f32[0:rows, :].astype(BF16).astype(F32)
    result_ref[:, cols] = (mixed * silu(gate_ref[:, cols].astype(F32))).astype(BF16)


def whole_kernel(
    x_hbm, gate_hbm, small_own, proj_own, step_own, result_ref,
    rows_ref, gate_ref, small_ref, proj_weight_ref, step_weight_ref,
    u_ref, rows_f32, in_wide, out_wide, out_half, step_ref, y_ref, end_ref, total_ref, chunk_carry,
    out1, in1, out2, in2, out3, in3, local_state, local_time,
    local_sem, halo_send, halo_recv, gather_send, gather_recv,
    send1, recv1, send2, recv2, send3, recv3,
):
    s, g = lax.axis_index("seq"), lax.axis_index("grp")
    seq, grp = lax.axis_size("seq"), lax.axis_size("grp")
    y, core = lax.div(g, 2), lax.rem(g, 2)
    y_left, y_right, y_far = lax.rem(y + 3, 4), lax.rem(y + 1, 4), lax.rem(y + 2, 4)
    group, x = lax.div(s, 4), lax.rem(s, 4)
    member = x * grp + g
    members, groups = 4 * grp, seq // 4
    flip = 4 - 8 * lax.rem(group, 2)
    right = (s + lax.div(y + 1, 4) * flip, y_right * 2 + core)
    left = (s + (1 - lax.div(y + 3, 4)) * flip, y_left * 2 + core)
    sibling = (s, y * 2 + 1 - core)
    place = s * grp + g
    count = seq * grp
    after, before = lax.rem(place + 1, count), lax.rem(place + count - 1, count)
    after, before = (lax.div(after, grp), lax.rem(after, grp)), (lax.div(before, grp), lax.rem(before, grp))

    def member_at(k):
        return (group * 4 + lax.div(k, grp), lax.rem(k, grp))

    def group_at(k):
        return (k * 4 + x, g)

    barrier = pltpu.get_barrier_semaphore()

    def greet(device):
        pl.semaphore_signal(barrier, inc=1, device_id=device, device_id_type=MESH)

    for device in (right, left, after, before):
        greet(device)

    def greet_member(d, _):
        greet(member_at(lax.rem(member + d, members)))
        return 0

    def greet_group(d, _):
        greet(group_at(lax.rem(group + d, groups)))
        return 0

    lax.fori_loop(1, members, greet_member, 0)
    lax.fori_loop(1, groups, greet_group, 0)
    pl.semaphore_wait(barrier, 4 + members - 1 + groups - 1)

    def remote(src, dst, send, recv, device):
        return pltpu.make_async_remote_copy(
            src_ref=src, dst_ref=dst, send_sem=send, recv_sem=recv, device_id=device,
            device_id_type=MESH,
        )

    rows = x_hbm.shape[0]
    halos = [
        remote(x_hbm.at[rows - HALO : rows], rows_ref.at[0:HALO], halo_send.at[0], halo_recv.at[0], after),
        remote(
            x_hbm.at[0:HALO], rows_ref.at[HALO + rows : 2 * HALO + rows], halo_send.at[1],
            halo_recv.at[1], before,
        ),
    ]
    own = (small_own, proj_own, step_own)
    whole = (small_ref, proj_weight_ref, step_weight_ref)
    locals_ = [
        pltpu.make_async_copy(x_hbm, rows_ref.at[HALO : HALO + rows], local_sem.at[0]),
        pltpu.make_async_copy(gate_hbm, gate_ref, local_sem.at[1]),
    ] + [pltpu.make_async_copy(own[c], whole[c].at[g], local_sem.at[2 + c]) for c in range(3)]

    def part(kind, slot, half):
        if half is None:
            return whole[kind].at[slot]
        if kind == 0:
            return whole[kind].at[slot, half * (ROWS_SMALL // 2) : (half + 1) * (ROWS_SMALL // 2)]
        return whole[kind].at[slot, half]

    sent_slot = (g, g, y_left * 2 + core, y_right * 2 + core, g, y_left * 2 + core,
                 y_right * 2 + core, y_far * 2 + core, y_far * 2 + core)
    other = 1 - core
    got_slot = (y_left * 2 + core, y_right * 2 + core, y_far * 2 + core, y_far * 2 + core,
                y * 2 + other, y_left * 2 + other, y_right * 2 + other, y_far * 2 + other,
                y_far * 2 + other)
    halves = (None, None, 0, 1, None, None, None, 0, 1)
    targets = (right, left, right, left) + (sibling,) * 5

    def outgoing(kind, way):
        dst = part(kind, sent_slot[way], halves[way])
        src = own[kind] if way in (0, 1, 4) else dst
        return remote(src, dst, gather_send.at[kind, way], gather_recv.at[kind, way], targets[way])

    def arrived(kind, way):
        dst = part(kind, got_slot[way], halves[way])
        remote(dst, dst, gather_send.at[kind, way], gather_recv.at[kind, way], targets[way]).wait_recv()

    def send_own(kind):
        for way in (0, 1, 4):
            outgoing(kind, way).start()

    def forward_near(kind):
        arrived(kind, 0)
        outgoing(kind, 2).start()
        outgoing(kind, 5).start()
        arrived(kind, 1)
        outgoing(kind, 3).start()
        outgoing(kind, 6).start()

    def forward_far(kind):
        arrived(kind, 2)
        outgoing(kind, 7).start()
        arrived(kind, 3)
        outgoing(kind, 8).start()

    locals_[2].start()
    send_own(0)
    for copy in halos:
        copy.start()
    locals_[0].start()
    locals_[3].start()
    send_own(1)
    locals_[4].start()
    locals_[1].start()

    first = jnp.where(place == 0, 0.0, 1.0).astype(F32)
    last = jnp.where(place == count - 1, 0.0, 1.0).astype(F32)
    tiles_chip = 8

    def conv_chip(chip):
        def body(i, _):
            convolve(chip * tiles_chip + i, rows_ref, first, last, small_ref, u_ref, rows_f32)
            return 0

        lax.fori_loop(0, tiles_chip, body, 0)

    forward_near(0)
    locals_[0].wait()
    for copy in halos:
        copy.wait_recv()
    locals_[2].wait()
    arrived(0, 4)
    conv_chip(y)
    arrived(0, 5)
    conv_chip(y_left)
    forward_far(0)
    arrived(0, 6)
    conv_chip(y_right)
    arrived(0, 7)
    arrived(0, 8)
    conv_chip(y_far)

    width = proj_weight_ref.shape[-1]

    def project(chip, totals):
        new = []
        for branch in range(2):
            total = totals[branch]
            for i in range(2):
                shard = chip * 2 + i
                cols = pl.ds(pl.multiple_of(shard * width, width), width)
                total = total + dot_t(u_ref[branch, :, cols], proj_weight_ref[shard, branch])
            new.append(total)
        return new

    forward_near(1)
    send_own(2)
    locals_[3].wait()
    arrived(1, 4)
    totals = [jnp.zeros((rows, proj_weight_ref.shape[2]), F32)] * 2
    totals = project(y, totals)
    arrived(1, 5)
    totals = project(y_left, totals)
    forward_far(1)
    arrived(1, 6)
    totals = project(y_right, totals)
    arrived(1, 7)
    arrived(1, 8)
    totals = project(y_far, totals)
    lows = []
    for branch in range(2):
        projected = totals[branch].astype(BF16)
        spread_maps(branch, projected[:, 128:160], in_wide, out_wide, out_half)
        lows.append(projected[:, 0:128])

    def stage(branch, chip, fresh):
        for i in range(2):
            step_sizes(branch, chip * 2 + i, lows[branch], step_weight_ref, small_ref, step_ref)

        def body(i, _):
            scan_tile(
                branch, chip * tiles_chip + i, u_ref, small_ref, step_ref, in_wide, out_wide, y_ref,
                end_ref, total_ref, fresh,
            )
            return 0

        lax.fori_loop(0, tiles_chip, body, 0)

    tiles = 4 * tiles_chip

    def send_members(branch, source, target, send, recv):
        def body(d, _):
            k = lax.rem(member + d, members)
            remote(
                source.at[branch, k], target.at[branch, member], send.at[branch, d],
                recv.at[branch, d], member_at(k),
            ).start()
            return 0

        lax.fori_loop(1, members, body, 0)

    def await_members(branch, target, send, recv):
        def body(d, _):
            k = lax.rem(member + members - d, members)
            remote(
                target.at[branch, k], target.at[branch, k], send.at[branch, d], recv.at[branch, d],
                member_at(k),
            ).wait_recv()
            return 0

        lax.fori_loop(1, members, body, 0)

    def await_sent(branch, source, send, last):
        def body(d, _):
            remote(
                source, source, send.at[branch, d], send.at[branch, d], sibling
            ).wait_send()
            return 0

        lax.fori_loop(1, last, body, 0)

    def send_states(branch):
        def body(i, _):
            for q in range(4):
                device_state(branch, i * 4 + q, small_ref, end_ref, total_ref, out1)
            return 0

        lax.fori_loop(0, tiles // 4, body, 0)
        send_members(branch, out1, in1, send1, recv1)

    lanes = pl.ds(pl.multiple_of(lax.rem(member, 4) * LANES, LANES), LANES)

    def own_rates(branch):
        low = ROW_RATE + 16 * branch
        return small_ref[lax.div(member, 4), low : low + 16, lanes]

    def combine_members(branch):
        await_members(branch, in1, send1, recv1)
        in1[branch, member] = out1[branch, member]
        rates = own_rates(branch)
        state = jnp.zeros((16, LANES), F32)
        elapsed = jnp.zeros((1, LANES), F32)
        for j in range(members):
            k = j if branch == 0 else members - 1 - j
            local_state[branch, k] = state
            local_time[branch, k] = jnp.broadcast_to(elapsed, (8, LANES))
            gained, span = of_message(in1[branch, k])
            state = jnp.exp2(rates * span) * state + gained
            elapsed = elapsed + span
        out2[branch] = as_message(state, elapsed)

        def body(d, _):
            k = lax.rem(group + d, groups)
            remote(
                out2.at[branch], in2.at[branch, group], send2.at[branch, d], recv2.at[branch, d],
                group_at(k),
            ).start()
            return 0

        lax.fori_loop(1, groups, body, 0)

    def combine_groups(branch):
        def body(d, _):
            k = lax.rem(group + groups - d, groups)
            remote(
                in2.at[branch, k], in2.at[branch, k], send2.at[branch, d], recv2.at[branch, d],
                group_at(k),
            ).wait_recv()
            return 0

        lax.fori_loop(1, groups, body, 0)
        in2[branch, group] = out2[branch]
        rates = own_rates(branch)
        state = jnp.zeros((16, LANES), F32)
        for j in range(groups):
            k = j if branch == 0 else groups - 1 - j
            gained, span = of_message(in2[branch, k])
            new = jnp.exp2(rates * span) * state + gained
            state = jnp.where(k < group if branch == 0 else k > group, new, state)
        for k in range(members):
            out3[branch, k] = (
                jnp.exp2(rates * local_time[branch, k, 0:1, :]) * state + local_state[branch, k]
            ).astype(BF16)
        send_members(branch, out3, in3, send3, recv3)
        in3[branch, member] = out3[branch, member]

    def correct(branch, start, stop):
        def body(tile, _):
            correct_tile(
                branch, tile, small_ref, step_ref, end_ref, out_half, in3, y_ref, total_ref, chunk_carry
            )
            if branch == 1:
                gate_tile(tile, y_ref, gate_ref, result_ref, rows_f32)
            return 0

        lax.fori_loop(start, stop, body, 0)

    locals_[4].wait()
    arrived(2, 4)
    stage(0, y, True)
    forward_near(2)
    stage(1, y, False)
    arrived(2, 5)
    stage(0, y_left, True)
    forward_far(2)
    arrived(2, 6)
    stage(0, y_right, True)
    arrived(2, 7)
    arrived(2, 8)
    stage(0, y_far, True)
    send_states(0)
    stage(1, y_left, False)
    combine_members(0)
    stage(1, y_right, False)
    combine_groups(0)
    stage(1, y_far, False)
    send_states(1)
    await_members(0, in3, send3, recv3)
    correct(0, 0, tiles // 2)
    combine_members(1)
    correct(0, tiles // 2, tiles)
    combine_groups(1)
    locals_[1].wait()
    await_members(1, in3, send3, recv3)
    correct(1, 0, tiles)

    for copy in halos:
        copy.wait_send()
    for kind in range(3):
        for way in range(9):
            outgoing(kind, way).wait_send()
    for branch in range(2):
        await_sent(branch, out1.at[branch, 0], send1, members)
        await_sent(branch, out2.at[branch], send2, groups)
        await_sent(branch, out3.at[branch, 0], send3, members)


def run_whole(x, gate, small, proj_weight, step_weight):
    rows, channels = x.shape
    tiles, steps = channels // LANES, rows // CHUNKS
    shards = lax.axis_size("grp")
    members = 4 * shards
    groups = lax.axis_size("seq") // 4
    anywhere = pl.BlockSpec(memory_space=pl.ANY)
    vmem, dma = pltpu.VMEM, pltpu.SemaphoreType.DMA
    return pl.pallas_call(
        whole_kernel,
        out_shape=jax.ShapeDtypeStruct((rows, channels), BF16),
        in_specs=[anywhere] * 5,
        out_specs=pl.BlockSpec(memory_space=pltpu.VMEM),
        scratch_shapes=[
            vmem((rows + 2 * HALO, channels), BF16),
            vmem((rows, channels), BF16),
            vmem((shards,) + small.shape, F32),
            vmem((shards,) + proj_weight.shape, BF16),
            vmem((shards,) + step_weight.shape, BF16),
            vmem((2, rows, channels), BF16),
            vmem((rows + 2 * HALO, LANES), F32),
            vmem((2, rows * 16, LANES), F32),
            vmem((2, rows * 16, LANES), F32),
            vmem((2, rows * 16, LANES), BF16),
            vmem((2, tiles, steps, CHUNKS, LANES), F32),
            vmem((tiles, steps, CHUNKS, LANES), F32),
            vmem((2, tiles, 16 * CHUNKS, LANES), F32),
            vmem((2, tiles, CHUNKS, LANES), F32),
            vmem((16 * CHUNKS, LANES), F32),
            vmem((2, members, 32, LANES), BF16),
            vmem((2, members, 32, LANES), BF16),
            vmem((2, 32, LANES), BF16),
            vmem((2, groups, 32, LANES), BF16),
            vmem((2, members, 16, LANES), BF16),
            vmem((2, members, 16, LANES), BF16),
            vmem((2, members, 16, LANES), F32),
            vmem((2, members, 8, LANES), F32),
            dma((5,)),
            dma((2,)),
            dma((2,)),
            dma((3, 9)),
            dma((3, 9)),
            dma((2, members)),
            dma((2, members)),
            dma((2, groups)),
            dma((2, groups)),
            dma((2, members)),
            dma((2, members)),
        ],
        compiler_params=pltpu.CompilerParams(
            vmem_limit_bytes=56 << 20, collective_id=0, has_side_effects=True
        ),
    )(x, gate, small, proj_weight, step_weight)


def local(
    inner_input,
    inner_gate,
    conv_weight,
    conv_bias,
    proj_weight,
    step_weight,
    step_bias,
    decay_rate,
    skip_gain,
):
    width = conv_weight.shape[2]
    small = jnp.concatenate(
        [
            conv_weight.reshape(8, width),
            conv_bias,
            step_bias,
            skip_gain,
            jnp.zeros((2, width), F32),
            decay_rate.reshape(32, width) * -LOG2E,
        ],
        0,
    )
    return run_whole(inner_input, inner_gate, small, jnp.swapaxes(proj_weight, 1, 2), step_weight)


def solution(mesh):
    placed = (
        P(("seq", "grp"), None),
        P(("seq", "grp"), None),
        P(None, None, "grp"),
        P(None, "grp"),
        P(None, "grp", None),
        P(None, None, "grp"),
        P(None, "grp"),
        P(None, None, "grp"),
        P(None, "grp"),
    )
    return jax.shard_map(
        local, mesh=mesh, in_specs=placed, out_specs=P(("seq", "grp"), None), check_vma=False
    )
```

time: 503 us -> 117 us (0.23)
  waiting for transfers between devices: 231 us -> 0 us
  local copies, waits for them, and re-layouts: 128 us -> 5.54 us
  Pallas kernels: 58.6 us -> 111 us
  blocking collectives: 42 us -> 0 us
  starting transfers between devices: 15.9 us -> 0 us
  between operations: 13.3 us -> 0.04 us
    all_gather x3 -> x0, waiting for transfers between devices: 215 us -> none  [the longest x1 150 us: entering_states(): everything = lax.all_gather(jnp.stack(totals), 'seq')]
    squeeze x129 -> x0, local copies, waits for them, and re-layouts: 116 us -> none  [the longest x128 116 us: turn(): return jnp.where(reached, through(carry, everything[at], branch), carry)]
    pallas_call x2 -> x1, Pallas kernels: 58.6 us -> 111 us  [run_whole(): pl.pallas_call(whole_kernel, out_shape=jax.ShapeDtypeStruct((rows, channe...]
    all_to_all x1 -> x0, blocking collectives: 24.3 us -> none  [entering_states(): back = lax.all_to_all(back, 'grp', split_axis=0, concat_axis=0, tiled=True)]
    all_gather x1 -> x0, blocking collectives: 17.7 us -> none  [local(): small = lax.all_gather(small, 'grp')]
    all_to_all x1 -> x0, waiting for transfers between devices: 15.2 us -> none  [entering_states(): both = lax.all_to_all(both, 'grp', split_axis=0, concat_axis=0, tiled=True)]
    ppermute x2 -> x0, starting transfers between devices: 10.1 us -> none  [the longest x1 5.49 us: local(): lax.ppermute(inner_input[:16], axes, [(i + 1, i) for i in range(count - 1)])]
    all_to_all x1 -> x0, starting transfers between devices: 5.79 us -> none  [entering_states(): both = lax.all_to_all(both, 'grp', split_axis=0, concat_axis=0, tiled=True)]
  transfers between devices with their start and end apart: 6 -> 0, of which waited for: 4 -> 0; matrix products, arithmetic and copies ran while one was open for 1% -> 0% of each run, Pallas kernels for 0% -> 0%
where the time goes in v2:
time: 117 us
  Pallas kernels  111 us (95%)
  local copies, waits for them, and re-layouts  5.54 us (5%)
    pallas_call x1, Pallas kernels, run_whole(): pl.pallas_call(whole_kernel, out_shape=jax.ShapeDtypeStruct((rows, channe...  111 us
    unnamed x7, local copies, waits for them, and re-layouts  2.95 us

profile of v2, /device:TPU:1, one launch (start us, length us, event | category | flops | bytes accessed | tf_op | source)
XLA Modules:
  0.0 117.2 jit_solution(3262002183311637956)
XLA Ops:
  0.0 0.7 reshape.6
  0.7 0.0 copy-start.1
  0.7 0.0 copy-start.2
  0.7 0.9 broadcast_multiply_fusion
  1.6 0.0 copy-start
  1.6 0.0 copy-done.1
  1.6 0.0 copy-done.2
  1.6 0.7 copy-done
  2.3 1.9 %concatenate.3.small_own = f32[48,512]{1,0:T(8,128)} concatenate(f32[8,512]{1,0:T(8,128)S(1)} %reshape.6, f32[2,512]{1,0:T(2,128)S(1)} %copy-done, f32[2,512]{1,0:T(2,128)S(1)} %copy-done.1, f32[2,512]{1,0:T(2,128)S(1)} %copy-done.2, f32[2,512]{1,0:T(2,128)S(1)} %broadcast_in_dim.3, f32[32,512]{1,0:T(8,128)S(1)} %bitcast.3), dimensions={0} | concatenate | bytes 196608 | tf_op jit(solution)/shard_map/concatenate | solution.py:662
  4.2 110.8 %shard_map.91 = bf16[128,4096]{1,0:T(8,128)(2,1)} custom-call(bf16[128,4096]{1,0:T(8,128)(2,1)} %x_hbm.1, bf16[128,4096]{1,0:T(8,128)(2,1)} %gate_hbm.1, f32[48,512]{1,0:T(8,128)} %concatenate.3.small_own, bf16[2,160,512]{2,1,0:T(8,128)(2,1)} %bitcast.2, bf16[2,128,512]{2,1,0:T(8,128)(2,1)} %step_own.1), custom_call_target="tpu_custom_call" | custom-call | tf_op jit(solution)/shard_map/pallas_call | solution.py:603
  114.9 2.3 %copy.11 = bf16[128,4096]{1,0:T(8,128)(2,1)} copy(bf16[128,4096]{1,0:T(8,128)(2,1)} %shard_map.91) | data formatting | bytes 2097152
  (1 shorter events, 0.0 us)
Async XLA Ops:
  0.7 0.9 copy-start.1
  0.7 0.9 copy-start.2
  1.6 0.7 copy-start

commit v3 on v2

v3 whole, which is shorter than its diff:
```python
import functools
import math

import jax
import jax.numpy as jnp
from jax import lax
from jax.experimental import pallas as pl
from jax.experimental.pallas import tpu as pltpu
from jax.sharding import PartitionSpec as P

F32 = jnp.float32
BF16 = jnp.bfloat16
LOG2E = math.log2(math.e)
LN2 = math.log(2.0)

CHUNKS = 8
LANES = 128

ROW_CONV = 0
ROW_BIAS = 8
ROWS_CONV = 16
ROW_STEP = 0
ROW_SKIP = 2
ROW_RATE = 8
ROWS_REST = 40
HALO = 16
MESH = pl.DeviceIdType.MESH


def iota(shape, dim):
    return lax.broadcasted_iota(jnp.int32, shape, dim)


def silu(value):
    half = 0.5 * value
    return half + half * jnp.tanh(half)


def softplus(value):
    small = jnp.exp2(jnp.abs(value) * -LOG2E)
    one_more = 1.0 + small
    return jnp.maximum(value, 0.0) + (LN2 * jnp.log2(one_more) + (small - (one_more - 1.0)))


def dot_t(a, b):
    return lax.dot_general(a, b, (((1,), (1,)), ((), ())), preferred_element_type=F32)


def convolve(tile, rows_ref, first, last, conv_ref, u_ref, rows_f32):
    rows = rows_ref.shape[0] - 2 * HALO
    steps = rows // CHUNKS
    shard, column = lax.div(tile, 4), lax.rem(tile, 4)
    cols = pl.ds(pl.multiple_of(tile * LANES, LANES), LANES)
    lanes = pl.ds(pl.multiple_of(column * LANES, LANES), LANES)
    rows_f32[0:HALO, :] = rows_ref[0:HALO, cols].astype(F32) * first
    rows_f32[HALO : HALO + rows, :] = rows_ref[HALO : HALO + rows, cols].astype(F32)
    rows_f32[HALO + rows : 2 * HALO + rows, :] = (
        rows_ref[HALO + rows : 2 * HALO + rows, cols].astype(F32) * last
    )
    taps = {t: rows_f32[pl.ds(HALO + t, CHUNKS, stride=steps), :] for t in range(-3, steps + 3)}
    for branch in range(2):
        weights = [
            jnp.broadcast_to(
                conv_ref[shard, ROW_CONV + 4 * branch + j : ROW_CONV + 4 * branch + j + 1, lanes],
                (CHUNKS, LANES),
            )
            for j in range(4)
        ]
        bias = jnp.broadcast_to(
            conv_ref[shard, ROW_BIAS + branch : ROW_BIAS + branch + 1, lanes], (CHUNKS, LANES)
        )
        sign = -1 if branch == 0 else 1
        for t in range(0, steps, 2):
            pair = []
            for s in (t, t + 1):
                total = bias
                for j in range(4):
                    total = total + weights[j] * taps[s + sign * (3 - j)]
                pair.append(silu(total))
            u_ref[branch, t * CHUNKS : (t + 2) * CHUNKS, cols] = jnp.concatenate(pair, 0).astype(
                BF16
            )


def spread_maps(branch, maps, in_wide, out_wide, out_half):
    rows = maps.shape[0]
    steps = rows // CHUNKS
    count = rows * 16
    tiles = maps.astype(F32).reshape(steps, 1, CHUNKS, 32)
    tiles = jnp.broadcast_to(tiles, (steps, 16, CHUNKS, 32)).reshape(count, 32)
    state = (iota((count, 32), 0) >> 3) & 15
    picked = jnp.where(state == (iota((count, 32), 1) & 15), tiles, 0.0).astype(BF16)
    ones = ((iota((32, 2 * LANES), 0) >> 4) == (iota((32, 2 * LANES), 1) >> 7)).astype(F32).astype(BF16)
    wide = jnp.dot(picked, ones, preferred_element_type=F32)
    in_wide[branch] = wide[:, :LANES]
    out_wide[branch] = wide[:, LANES:]
    pairs = wide[:, LANES:].reshape(steps // 2, 2, 16, CHUNKS, LANES)
    for pair in range(steps // 2):
        both = jnp.concatenate([pairs[pair, 0], pairs[pair, 1]], 1)
        out_half[branch, pair * 256 : (pair + 1) * 256, :] = both.reshape(256, LANES).astype(BF16)


def step_sizes(branch, shard, low, step_weight_ref, rest_ref, step_ref):
    width = step_weight_ref.shape[-1]
    rows = low.shape[0]
    value = jnp.dot(low, step_weight_ref[shard, branch], preferred_element_type=F32)
    value = softplus(value + rest_ref[shard, ROW_STEP + branch : ROW_STEP + branch + 1, :])
    for q in range(width // LANES):
        step_ref[branch, shard * (width // LANES) + q] = value[
            :, q * LANES : (q + 1) * LANES
        ].reshape(rows // CHUNKS, CHUNKS, LANES)


def scan_tile(
    branch, tile, u_ref, rest_ref, step_ref, in_wide, out_wide, y_ref, end_ref, total_ref, fresh
):
    steps = step_ref.shape[2]
    shard, column = lax.div(tile, 4), lax.rem(tile, 4)
    cols = pl.ds(pl.multiple_of(tile * LANES, LANES), LANES)
    lanes = pl.ds(pl.multiple_of(column * LANES, LANES), LANES)
    first = ROW_RATE + 16 * branch
    skip = jnp.broadcast_to(
        rest_ref[shard, ROW_SKIP + branch : ROW_SKIP + branch + 1, lanes], (CHUNKS, LANES)
    )
    for start in (0, 8):
        rates = jnp.stack(
            [
                jnp.broadcast_to(
                    rest_ref[shard, first + n : first + n + 1, lanes], (CHUNKS, LANES)
                )
                for n in range(start, start + 8)
            ]
        )
        state = jnp.zeros((8, CHUNKS, LANES), F32)
        elapsed = jnp.zeros((CHUNKS, LANES), F32)
        for j in range(steps):
            t = j if branch == 0 else steps - 1 - j
            size = step_ref[branch, tile, t]
            u = u_ref[branch, pl.ds(t * CHUNKS, CHUNKS), cols].astype(F32)
            at = pl.ds((t * 16 + start) * CHUNKS, 8 * CHUNKS)
            into = in_wide[branch, at, :].reshape(8, CHUNKS, LANES)
            out = out_wide[branch, at, :].reshape(8, CHUNKS, LANES)
            state = jnp.exp2(rates * size[None]) * state + (size * u)[None] * into
            part = jnp.sum(out * state, axis=0)
            if start == 0:
                part = part + skip * u
                elapsed = elapsed + size
            if start > 0 or not fresh:
                part = part + y_ref[tile, t]
            y_ref[tile, t] = part
        if start == 0:
            total_ref[branch, tile] = elapsed
        end_ref[branch, tile, start * CHUNKS : (start + 8) * CHUNKS, :] = state.reshape(
            8 * CHUNKS, LANES
        )


def device_state(branch, tile, rest_ref, end_ref, total_ref):
    shard, column = lax.div(tile, 4), lax.rem(tile, 4)
    lanes = pl.ds(pl.multiple_of(column * LANES, LANES), LANES)
    first = ROW_RATE + 16 * branch
    rates = rest_ref[shard, first : first + 16, lanes]
    state = jnp.zeros((16, LANES), F32)
    elapsed = jnp.zeros((1, LANES), F32)
    for j in range(CHUNKS):
        k = j if branch == 0 else CHUNKS - 1 - j
        span = total_ref[branch, tile, k : k + 1, :]
        state = jnp.exp2(rates * span) * state + end_ref[branch, tile, pl.ds(k, 16, stride=CHUNKS), :]
        elapsed = elapsed + span
    return state, elapsed


def as_message(state, elapsed):
    high = elapsed.astype(BF16).astype(F32)
    low = elapsed - high
    row = iota((16, LANES), 0)
    times = jnp.where(row == 0, high, jnp.where(row == 1, low, 0.0))
    return jnp.concatenate([state, times], 0).astype(BF16)


def of_message(message):
    values = message.astype(F32)
    return values[0:16], values[16:17] + values[17:18]


def correct_tile(
    branch, tile, rest_ref, step_ref, end_ref, out_half, carry, y_ref, total_ref, chunk_carry
):
    shard, column = lax.div(tile, 4), lax.rem(tile, 4)
    lanes = pl.ds(pl.multiple_of(column * LANES, LANES), LANES)
    first = ROW_RATE + 16 * branch
    steps = step_ref.shape[2]
    rates = rest_ref[shard, first : first + 16, lanes]
    for j in range(CHUNKS):
        k = j if branch == 0 else CHUNKS - 1 - j
        chunk_carry[pl.ds(k, 16, stride=CHUNKS), :] = carry
        if j < CHUNKS - 1:
            carry = (
                jnp.exp2(rates * total_ref[branch, tile, k : k + 1, :]) * carry
                + end_ref[branch, tile, pl.ds(k, 16, stride=CHUNKS), :]
            )
    entering = []
    wide = []
    for n in range(16):
        one = chunk_carry[n * CHUNKS : (n + 1) * CHUNKS, :]
        entering.append(jnp.concatenate([one, one], 0).astype(BF16))
        rate = rest_ref[shard, first + n : first + n + 1, lanes]
        wide.append(jnp.broadcast_to(rate, (16, LANES)).astype(BF16))
    elapsed = jnp.zeros((CHUNKS, LANES), F32)
    for j in range(0, steps, 2):
        pair = []
        for i in (j, j + 1):
            t = i if branch == 0 else steps - 1 - i
            elapsed = elapsed + step_ref[branch, tile, t]
            pair.append(elapsed)
        low = j if branch == 0 else steps - 2 - j
        if branch == 1:
            pair = pair[::-1]
        spans = jnp.concatenate(pair, 0).astype(BF16)
        total = None
        for n in range(16):
            at = ((low // 2) * 16 + n) * 16
            part = jnp.exp2(wide[n] * spans) * entering[n] * out_half[branch, at : at + 16, :]
            total = part if total is None else total + part
        total = total.astype(F32)
        y_ref[tile, low] = y_ref[tile, low] + total[:CHUNKS]
        y_ref[tile, low + 1] = y_ref[tile, low + 1] + total[CHUNKS:]


def mix_tile(tile, y_ref, result_ref, rows_f32):
    steps = y_ref.shape[1]
    rows = result_ref.shape[0]
    cols = pl.ds(pl.multiple_of(tile * LANES, LANES), LANES)
    for t in range(steps):
        rows_f32[pl.ds(t, CHUNKS, stride=steps), :] = y_ref[tile, t]
    result_ref[:, cols] = rows_f32[0:rows, :].astype(BF16)


def whole_kernel(
    x_hbm, conv_own, bias_own, proj_own, step_own, shift_own, rate_own, skip_own, result_ref,
    rows_ref, conv_in, bias_in, shift_in, rate_in, skip_in,
    conv_ref, proj_weight_ref, rest_ref, step_weight_ref,
    u_ref, rows_f32, in_wide, out_wide, out_half, step_ref, y_ref, end_ref, total_ref, chunk_carry,
    mine_state, mine_time, out0, in0, out1, in1, out2, in2, out3, in3, out4, in4, own_carry,
    local_state, local_time,
    local_sem, halo_send, halo_recv, gather_send, gather_recv,
    send0, recv0, send1, recv1, send2, recv2, send3, recv3, send4, recv4,
):
    s, g = lax.axis_index("seq"), lax.axis_index("grp")
    seq, grp = lax.axis_size("seq"), lax.axis_size("grp")
    y, core = lax.div(g, 2), lax.rem(g, 2)
    other = 1 - core
    y_left, y_right, y_far = lax.rem(y + 3, 4), lax.rem(y + 1, 4), lax.rem(y + 2, 4)
    group, x = lax.div(s, 4), lax.rem(s, 4)
    chip = x * 4 + y
    chips, groups = 16, seq // 4
    flip = 4 - 8 * lax.rem(group, 2)
    right = (s + lax.div(y + 1, 4) * flip, y_right * 2 + core)
    left = (s + (1 - lax.div(y + 3, 4)) * flip, y_left * 2 + core)
    sibling = (s, y * 2 + other)
    place = s * grp + g
    count = seq * grp
    after, before = lax.rem(place + 1, count), lax.rem(place + count - 1, count)
    after, before = (lax.div(after, grp), lax.rem(after, grp)), (lax.div(before, grp), lax.rem(before, grp))

    def chip_at(k):
        return (group * 4 + lax.div(k, 4), lax.rem(k, 4) * 2 + core)

    def group_at(k):
        return (k * 4 + x, g)

    def remote(src, dst, send, recv, device):
        return pltpu.make_async_remote_copy(
            src_ref=src, dst_ref=dst, send_sem=send, recv_sem=recv, device_id=device,
            device_id_type=MESH,
        )

    rows = x_hbm.shape[0]
    small_copies = [
        pltpu.make_async_copy(src, dst, local_sem.at[k])
        for k, (src, dst) in enumerate(
            [(conv_own, conv_in), (bias_own, bias_in), (shift_own, shift_in), (rate_own, rate_in),
             (skip_own, skip_in)]
        )
    ]
    rows_copy = pltpu.make_async_copy(x_hbm, rows_ref.at[HALO : HALO + rows], local_sem.at[5])
    proj_copy = pltpu.make_async_copy(proj_own, proj_weight_ref.at[g], local_sem.at[6])
    step_copy = pltpu.make_async_copy(step_own, step_weight_ref.at[g], local_sem.at[7])
    for copy in small_copies:
        copy.start()
    rows_copy.start()
    proj_copy.start()
    step_copy.start()

    barrier = pltpu.get_barrier_semaphore()

    def greet(device):
        pl.semaphore_signal(barrier, inc=1, device_id=device, device_id_type=MESH)

    for device in (right, left, after, before, sibling):
        greet(device)
    for d in range(1, chips):
        greet(chip_at(lax.rem(chip + d, chips)))
    for d in range(1, groups):
        greet(group_at(lax.rem(group + d, groups)))

    for copy in small_copies:
        copy.wait()
    width = conv_in.shape[-1]
    conv_ref[g, 0:4, :] = conv_in[0]
    conv_ref[g, 4:8, :] = conv_in[1]
    conv_ref[g, 8:10, :] = bias_in[...]
    conv_ref[g, 10:16, :] = jnp.zeros((6, width), F32)
    rest_ref[g, 0:2, :] = shift_in[...]
    rest_ref[g, 2:4, :] = skip_in[...]
    rest_ref[g, 4:8, :] = jnp.zeros((4, width), F32)
    rest_ref[g, 8:24, :] = rate_in[0] * -LOG2E
    rest_ref[g, 24:40, :] = rate_in[1] * -LOG2E
    pl.semaphore_wait(barrier, 5 + chips - 1 + groups - 1)

    halos = [
        remote(x_hbm.at[rows - HALO : rows], rows_ref.at[0:HALO], halo_send.at[0], halo_recv.at[0], after),
        remote(
            x_hbm.at[0:HALO], rows_ref.at[HALO + rows : 2 * HALO + rows], halo_send.at[1],
            halo_recv.at[1], before,
        ),
    ]
    whole = (conv_ref, proj_weight_ref, rest_ref, step_weight_ref)
    own = (conv_ref.at[g], proj_own, rest_ref.at[g], step_own)
    cuts = ((0, 8, 16), None, (0, 24, 40), None)

    def part(kind, slot, half):
        if half is None:
            return whole[kind].at[slot]
        if cuts[kind] is not None:
            return whole[kind].at[slot, cuts[kind][half] : cuts[kind][half + 1]]
        return whole[kind].at[slot, half]

    sent_slot = (g, g, y_left * 2 + core, y_right * 2 + core, g, y_left * 2 + core,
                 y_right * 2 + core, y_far * 2 + core, y_far * 2 + core)
    got_slot = (y_left * 2 + core, y_right * 2 + core, y_far * 2 + core, y_far * 2 + core,
                y * 2 + other, y_left * 2 + other, y_right * 2 + other, y_far * 2 + other,
                y_far * 2 + other)
    halves = (None, None, 0, 1, None, None, None, 0, 1)
    targets = (right, left, right, left) + (sibling,) * 5

    def outgoing(kind, way):
        dst = part(kind, sent_slot[way], halves[way])
        src = own[kind] if way in (0, 1, 4) else dst
        return remote(src, dst, gather_send.at[kind, way], gather_recv.at[kind, way], targets[way])

    def arrived(kind, way):
        dst = part(kind, got_slot[way], halves[way])
        remote(dst, dst, gather_send.at[kind, way], gather_recv.at[kind, way], targets[way]).wait_recv()

    def send_own(kind):
        for way in (0, 1, 4):
            outgoing(kind, way).start()

    def forward_near(kind):
        arrived(kind, 0)
        outgoing(kind, 2).start()
        outgoing(kind, 5).start()
        arrived(kind, 1)
        outgoing(kind, 3).start()
        outgoing(kind, 6).start()

    def forward_far(kind):
        arrived(kind, 2)
        outgoing(kind, 7).start()
        arrived(kind, 3)
        outgoing(kind, 8).start()

    send_own(0)
    for copy in halos:
        copy.start()
    send_own(1)

    first = jnp.where(place == 0, 0.0, 1.0).astype(F32)
    last = jnp.where(place == count - 1, 0.0, 1.0).astype(F32)
    tiles_chip = 8

    def conv_chip(at):
        def body(i, _):
            convolve(at * tiles_chip + i, rows_ref, first, last, conv_ref, u_ref, rows_f32.at[0])
            return 0

        lax.fori_loop(0, tiles_chip, body, 0)

    forward_near(0)
    rows_copy.wait()
    for copy in halos:
        copy.wait_recv()
    arrived(0, 4)
    conv_chip(y)
    arrived(0, 5)
    conv_chip(y_left)
    forward_far(0)
    arrived(0, 6)
    conv_chip(y_right)
    arrived(0, 7)
    arrived(0, 8)
    conv_chip(y_far)

    def project(at, totals):
        new = []
        for branch in range(2):
            total = totals[branch]
            for i in range(2):
                shard = at * 2 + i
                cols = pl.ds(pl.multiple_of(shard * width, width), width)
                total = total + dot_t(u_ref[branch, :, cols], proj_weight_ref[shard, branch])
            new.append(total)
        return new

    forward_near(1)
    send_own(2)
    send_own(3)
    proj_copy.wait()
    arrived(1, 4)
    totals = [jnp.zeros((rows, proj_weight_ref.shape[2]), F32)] * 2
    totals = project(y, totals)
    arrived(1, 5)
    totals = project(y_left, totals)
    forward_far(1)
    arrived(1, 6)
    totals = project(y_right, totals)
    arrived(1, 7)
    arrived(1, 8)
    totals = project(y_far, totals)
    lows = []
    for branch in range(2):
        projected = totals[branch].astype(BF16)
        spread_maps(branch, projected[:, 128:160], in_wide, out_wide, out_half)
        lows.append(projected[:, 0:128])

    def steps_of(branch, at):
        for i in range(2):
            step_sizes(branch, at * 2 + i, lows[branch], step_weight_ref, rest_ref, step_ref)

    def scan(branch, at):
        def body(i, _):
            scan_tile(
                branch, at * tiles_chip + i, u_ref, rest_ref, step_ref, in_wide, out_wide, y_ref,
                end_ref, total_ref, branch == 0,
            )
            return 0

        lax.fori_loop(0, tiles_chip, body, 0)

    def to_core(branch, at):
        span = pl.ds(at * 4, 4)
        return remote(
            out0.at[branch, span], in0.at[branch, span], send0.at[branch, at], recv0.at[branch, at],
            sibling,
        )

    def finish(branch, at):
        for i in range(4):
            k = at * 4 + i
            state, elapsed = device_state(branch, 2 * k + core, rest_ref, end_ref, total_ref)
            mine_state[branch, k] = state
            mine_time[branch, k] = jnp.broadcast_to(elapsed, (8, LANES))
            out0[branch, k] = as_message(
                *device_state(branch, 2 * k + other, rest_ref, end_ref, total_ref)
            )
        to_core(branch, at).start()

    def rates_of(branch, k):
        tile = 2 * k + core
        low = ROW_RATE + 16 * branch
        lanes = pl.ds(pl.multiple_of(lax.rem(tile, 4) * LANES, LANES), LANES)
        return rest_ref[lax.div(tile, 4), low : low + 16, lanes]

    def in_order(branch, k):
        here = (mine_state[branch, k], mine_time[branch, k, 0:1, :])
        there = of_message(in0[branch, k])
        leads = core == branch
        return [
            jnp.where(leads, a, b)
            for a, b in ((here[0], there[0]), (here[1], there[1]), (there[0], here[0]), (there[1], here[1]))
        ]

    def to_chip(branch, k):
        return remote(
            out1.at[branch, k], in1.at[branch, chip], send1.at[branch, k], recv1.at[branch, chip],
            chip_at(k),
        )

    def relay(branch, at):
        to_core(branch, at).wait_recv()
        for i in range(4):
            k = at * 4 + i
            state1, time1, state2, time2 = in_order(branch, k)
            state = jnp.exp2(rates_of(branch, k) * time2) * state1 + state2
            out1[branch, k] = as_message(state, time1 + time2)
        for i in range(4):
            k = at * 4 + i

            @pl.when(k != chip)
            def _():
                to_chip(branch, k).start()

    def combine_chips(branch):
        for d in range(1, chips):
            k = lax.rem(chip + chips - d, chips)
            remote(
                in1.at[branch, k], in1.at[branch, k], send1.at[branch, k], recv1.at[branch, k], chip_at(k)
            ).wait_recv()
        in1[branch, chip] = out1[branch, chip]
        rates = rates_of(branch, chip)
        state = jnp.zeros((16, LANES), F32)
        elapsed = jnp.zeros((1, LANES), F32)
        for j in range(chips):
            k = j if branch == 0 else chips - 1 - j
            local_state[branch, k] = state
            local_time[branch, k] = jnp.broadcast_to(elapsed, (8, LANES))
            gained, span = of_message(in1[branch, k])
            state = jnp.exp2(rates * span) * state + gained
            elapsed = elapsed + span
        out2[branch] = as_message(state, elapsed)
        for d in range(1, groups):
            k = lax.rem(group + d, groups)
            remote(
                out2.at[branch], in2.at[branch, group], send2.at[branch, k], recv2.at[branch, group],
                group_at(k),
            ).start()

    def combine_groups(branch):
        for d in range(1, groups):
            k = lax.rem(group + groups - d, groups)
            remote(
                in2.at[branch, k], in2.at[branch, k], send2.at[branch, k], recv2.at[branch, k], group_at(k)
            ).wait_recv()
        in2[branch, group] = out2[branch]
        rates = rates_of(branch, chip)
        state = jnp.zeros((16, LANES), F32)
        for j in range(groups):
            k = j if branch == 0 else groups - 1 - j
            gained, span = of_message(in2[branch, k])
            new = jnp.exp2(rates * span) * state + gained
            state = jnp.where(k < group if branch == 0 else k > group, new, state)
        for k in range(chips):
            out3[branch, k] = (
                jnp.exp2(rates * local_time[branch, k, 0:1, :]) * state + local_state[branch, k]
            ).astype(BF16)
        for d in range(1, chips):
            k = lax.rem(chip + d, chips)
            remote(
                out3.at[branch, k], in3.at[branch, chip], send3.at[branch, k], recv3.at[branch, chip],
                chip_at(k),
            ).start()

    def back_to_core(branch):
        return remote(out4.at[branch], in4.at[branch], send4.at[branch], recv4.at[branch], sibling)

    def receive(branch):
        for d in range(1, chips):
            k = lax.rem(chip + chips - d, chips)
            remote(
                in3.at[branch, k], in3.at[branch, k], send3.at[branch, k], recv3.at[branch, k], chip_at(k)
            ).wait_recv()
        in3[branch, chip] = out3[branch, chip]
        leads = core == branch
        for k in range(chips):
            carry = in3[branch, k].astype(F32)
            state1, time1, _, _ = in_order(branch, k)
            second = jnp.exp2(rates_of(branch, k) * time1) * carry + state1
            own_carry[branch, k] = jnp.where(leads, carry, second).astype(BF16)
            out4[branch, k] = jnp.where(leads, second, carry).astype(BF16)
        back_to_core(branch).start()

    def correct(branch, mine, start, stop):
        held = own_carry if mine else in4

        def body(i, _):
            for q in range(2):
                k = 2 * i + q
                tile = 2 * k + (core if mine else other)
                correct_tile(
                    branch, tile, rest_ref, step_ref, end_ref, out_half, held[branch, k].astype(F32),
                    y_ref, total_ref, chunk_carry.at[q],
                )
                if branch == 1:
                    mix_tile(tile, y_ref, result_ref, rows_f32.at[q])
            return 0

        lax.fori_loop(start // 2, stop // 2, body, 0)

    step_copy.wait()
    arrived(2, 4)
    arrived(3, 4)
    steps_of(0, y)
    scan(0, y)
    finish(0, y)
    forward_near(2)
    forward_near(3)
    steps_of(1, y)
    relay(0, y)
    scan(1, y)
    finish(1, y)
    arrived(2, 5)
    arrived(3, 5)
    steps_of(0, y_left)
    relay(1, y)
    scan(0, y_left)
    finish(0, y_left)
    forward_far(2)
    forward_far(3)
    arrived(2, 6)
    arrived(3, 6)
    steps_of(0, y_right)
    relay(0, y_left)
    scan(0, y_right)
    finish(0, y_right)
    for kind in (2, 3):
        for way in (7, 8):
            arrived(kind, way)
    steps_of(0, y_far)
    relay(0, y_right)
    scan(0, y_far)
    finish(0, y_far)
    steps_of(1, y_left)
    relay(0, y_far)
    scan(1, y_left)
    finish(1, y_left)
    combine_chips(0)
    steps_of(1, y_right)
    relay(1, y_left)
    scan(1, y_right)
    finish(1, y_right)
    combine_groups(0)
    steps_of(1, y_far)
    relay(1, y_right)
    scan(1, y_far)
    finish(1, y_far)
    receive(0)
    relay(1, y_far)
    correct(0, True, 0, 8)
    combine_chips(1)
    correct(0, True, 8, 16)
    back_to_core(0).wait_recv()
    correct(0, False, 0, 8)
    combine_groups(1)
    correct(0, False, 8, 16)
    receive(1)
    correct(1, True, 0, 16)
    back_to_core(1).wait_recv()
    correct(1, False, 0, 16)

    for copy in halos:
        copy.wait_send()
    for kind in range(4):
        for way in range(9):
            outgoing(kind, way).wait_send()
    for branch in range(2):
        for at in range(4):
            to_core(branch, at).wait_send()
        back_to_core(branch).wait_send()
        for d in range(1, chips):
            k = lax.rem(chip + d, chips)
            for source, send in ((out1, send1), (out3, send3)):
                remote(
                    source.at[branch, k], source.at[branch, k], send.at[branch, k], recv1.at[branch, k],
                    chip_at(k),
                ).wait_send()
        for d in range(1, groups):
            k = lax.rem(group + d, groups)
            remote(
                out2.at[branch], out2.at[branch], send2.at[branch, k], recv2.at[branch, k], group_at(k)
            ).wait_send()


def run_whole(x, conv_weight, conv_bias, proj_weight, step_weight, step_bias, decay_rate, skip_gain):
    rows, channels = x.shape
    width = conv_weight.shape[2]
    tiles, steps = channels // LANES, rows // CHUNKS
    shards = lax.axis_size("grp")
    chips = 2 * shards
    groups = lax.axis_size("seq") // 4
    anywhere = pl.BlockSpec(memory_space=pl.ANY)
    vmem, dma = pltpu.VMEM, pltpu.SemaphoreType.DMA
    return pl.pallas_call(
        whole_kernel,
        out_shape=jax.ShapeDtypeStruct((rows, channels), BF16),
        in_specs=[anywhere] * 8,
        out_specs=pl.BlockSpec(memory_space=pltpu.VMEM),
        scratch_shapes=[
            vmem((rows + 2 * HALO, channels), BF16),
            vmem(conv_weight.shape, F32),
            vmem(conv_bias.shape, F32),
            vmem(step_bias.shape, F32),
            vmem(decay_rate.shape, F32),
            vmem(skip_gain.shape, F32),
            vmem((shards, ROWS_CONV, width), F32),
            vmem((shards,) + proj_weight.shape, BF16),
            vmem((shards, ROWS_REST, width), F32),
            vmem((shards,) + step_weight.shape, BF16),
            vmem((2, rows, channels), BF16),
            vmem((2, rows + 2 * HALO, LANES), F32),
            vmem((2, rows * 16, LANES), F32),
            vmem((2, rows * 16, LANES), F32),
            vmem((2, rows * 16, LANES), BF16),
            vmem((2, tiles, steps, CHUNKS, LANES), F32),
            vmem((tiles, steps, CHUNKS, LANES), F32),
            vmem((2, tiles, 16 * CHUNKS, LANES), F32),
            vmem((2, tiles, CHUNKS, LANES), F32),
            vmem((2, 16 * CHUNKS, LANES), F32),
            vmem((2, chips, 16, LANES), F32),
            vmem((2, chips, 8, LANES), F32),
            vmem((2, chips, 32, LANES), BF16),
            vmem((2, chips, 32, LANES), BF16),
            vmem((2, chips, 32, LANES), BF16),
            vmem((2, chips, 32, LANES), BF16),
            vmem((2, 32, LANES), BF16),
            vmem((2, groups, 32, LANES), BF16),
            vmem((2, chips, 16, LANES), BF16),
            vmem((2, chips, 16, LANES), BF16),
            vmem((2, chips, 16, LANES), BF16),
            vmem((2, chips, 16, LANES), BF16),
            vmem((2, chips, 16, LANES), BF16),
            vmem((2, chips, 16, LANES), F32),
            vmem((2, chips, 8, LANES), F32),
            dma((8,)),
            dma((2,)),
            dma((2,)),
            dma((4, 9)),
            dma((4, 9)),
            dma((2, 4)),
            dma((2, 4)),
            dma((2, chips)),
            dma((2, chips)),
            dma((2, groups)),
            dma((2, groups)),
            dma((2, chips)),
            dma((2, chips)),
            dma((2,)),
            dma((2,)),
        ],
        compiler_params=pltpu.CompilerParams(
            vmem_limit_bytes=56 << 20, collective_id=0, has_side_effects=True
        ),
    )(x, conv_weight, conv_bias, proj_weight, step_weight, step_bias, decay_rate, skip_gain)


def local(
    inner_input,
    inner_gate,
    conv_weight,
    conv_bias,
    proj_weight,
    step_weight,
    step_bias,
    decay_rate,
    skip_gain,
):
    mixed = run_whole(
        inner_input, conv_weight, conv_bias, jnp.swapaxes(proj_weight, 1, 2), step_weight, step_bias,
        decay_rate, skip_gain,
    )
    return (mixed.astype(F32) * jax.nn.silu(inner_gate.astype(F32))).astype(BF16)


def solution(mesh):
    placed = (
        P(("seq", "grp"), None),
        P(("seq", "grp"), None),
        P(None, None, "grp"),
        P(None, "grp"),
        P(None, "grp", None),
        P(None, None, "grp"),
        P(None, "grp"),
        P(None, None, "grp"),
        P(None, "grp"),
    )
    return jax.shard_map(
        local, mesh=mesh, in_specs=placed, out_specs=P(("seq", "grp"), None), check_vma=False
    )
```

time: 117 us -> 105 us (0.90)
  Pallas kernels: 111 us -> 102 us
  local copies, waits for them, and re-layouts: 5.54 us -> 0.01 us
  other arithmetic: 0.87 us -> 2.83 us
    pallas_call x1, Pallas kernels: 111 us -> 102 us  [run_whole(): pl.pallas_call(whole_kernel, out_shape=jax.ShapeDtypeStruct((rows, channe...]
    unnamed x7 -> x2, local copies, waits for them, and re-layouts: 2.95 us -> 0.01 us
    convert_element_type x0 -> x1, other arithmetic: none -> 2.83 us  [local(): (mixed.astype(F32) * jax.nn.silu(inner_gate.astype(F32))).astype(BF16)]
    concatenate x1 -> x0, local copies, waits for them, and re-layouts: 1.86 us -> none  [local(): jnp.concatenate([conv_weight.reshape(8, width), conv_bias, step_bias, ski...]
where the time goes in v3:
time: 105 us
  Pallas kernels  102 us (97%)
  other arithmetic  2.83 us (3%)
    pallas_call x1, Pallas kernels, run_whole(): pl.pallas_call(whole_kernel, out_shape=jax.ShapeDtypeStruct((rows, channe...  102 us
    convert_element_type x1, other arithmetic, local(): (mixed.astype(F32) * jax.nn.silu(inner_gate.astype(F32))).astype(BF16)  2.83 us

profile of v3, /device:TPU:1, one launch (start us, length us, event | category | flops | bytes accessed | tf_op | source)
XLA Modules:
  0.0 104.6 jit_solution(18088070764155505866)
XLA Ops:
  0.0 0.0 copy-start
  0.0 101.8 %shard_map.91 = bf16[128,4096]{1,0:T(8,128)(2,1)} custom-call(bf16[128,4096]{1,0:T(8,128)(2,1)} %x_hbm.1, f32[2,4,512]{2,1,0:T(4,128)} %conv_own.1, f32[2,512]{1,0:T(2,128)} %bias_own.1, bf16[2,160,512]{2,1,0:T(8,128)(2,1)} %bitcast.1, bf16[2,128,512]{2,1,0:T(8,128)(2,1)} %step_own.1, f32[2,512]{1,0:T(2,128)} %shift_own.1, f32[2,16,512]{2,1,0:T(8,128)} %rate_own.1, ...), custom_call_target="tpu_custom_call" | custom-call | tf_op jit(solution)/shard_map/pallas_call | solution.py:683
  101.8 0.0 copy-done
  101.8 2.8 %fusion.4 = bf16[128,4096]{1,0:T(8,128)(2,1)} fusion(bf16[128,4096]{1,0:T(8,128)(2,1)S(1)} %copy-done, bf16[128,4096]{1,0:T(8,128)(2,1)} %shard_map.91), kind=kLoop, calls=%fused_computation.6 | loop fusion | flops 4194304 | bytes 3145728 | tf_op jit(solution)/shard_map/convert_element_type | solution.py:761
Async XLA Ops:
  0.0 101.8 %copy-start = (bf16[128,4096]{1,0:T(8,128)(2,1)S(1)}, bf16[128,4096]{1,0:T(8,128)(2,1)}, u32[]{:S(2)}) copy-start(bf16[128,4096]{1,0:T(8,128)(2,1)} %param.10) | copy-start | bytes 3145732

commit v4 on v3

--- a/solution.py
+++ b/solution.py
@@ -24,6 +24,7 @@
 ROW_RATE = 8
 ROWS_REST = 40
 HALO = 16
+DIRECT = (0, 1)
 MESH = pl.DeviceIdType.MESH
 
 
@@ -82,7 +83,7 @@
             )
 
 
-def spread_maps(branch, maps, in_wide, out_wide, out_half):
+def spread_maps(branch, maps, in_wide, out_wide, in_half, out_half):
     rows = maps.shape[0]
     steps = rows // CHUNKS
     count = rows * 16
@@ -94,10 +95,11 @@
     wide = jnp.dot(picked, ones, preferred_element_type=F32)
     in_wide[branch] = wide[:, :LANES]
     out_wide[branch] = wide[:, LANES:]
-    pairs = wide[:, LANES:].reshape(steps // 2, 2, 16, CHUNKS, LANES)
-    for pair in range(steps // 2):
-        both = jnp.concatenate([pairs[pair, 0], pairs[pair, 1]], 1)
-        out_half[branch, pair * 256 : (pair + 1) * 256, :] = both.reshape(256, LANES).astype(BF16)
+    for half, target in ((0, in_half), (1, out_half)):
+        pairs = wide[:, half * LANES : (half + 1) * LANES].reshape(steps // 2, 2, 16, CHUNKS, LANES)
+        for pair in range(steps // 2):
+            both = jnp.concatenate([pairs[pair, 0], pairs[pair, 1]], 1)
+            target[branch, pair * 256 : (pair + 1) * 256, :] = both.reshape(256, LANES).astype(BF16)
 
 
 def step_sizes(branch, shard, low, step_weight_ref, rest_ref, step_ref):
@@ -148,11 +150,46 @@
             if start > 0 or not fresh:
                 part = part + y_ref[tile, t]
             y_ref[tile, t] = part
-        if start == 0:
+        if start == 0 and fresh:
             total_ref[branch, tile] = elapsed
         end_ref[branch, tile, start * CHUNKS : (start + 8) * CHUNKS, :] = state.reshape(
             8 * CHUNKS, LANES
         )
+
+
+def chunk_states(branch, tile, u_ref, rest_ref, step_ref, in_half, end_ref, total_ref):
+    steps = step_ref.shape[2]
+    shard, column = lax.div(tile, 4), lax.rem(tile, 4)
+    cols = pl.ds(pl.multiple_of(tile * LANES, LANES), LANES)
+    lanes = pl.ds(pl.multiple_of(column * LANES, LANES), LANES)
+    first = ROW_RATE + 16 * branch
+    rates = [
+        jnp.broadcast_to(rest_ref[shard, first + n : first + n + 1, lanes], (16, LANES)).astype(BF16)
+        for n in range(16)
+    ]
+    states = [None] * 16
+    left = jnp.zeros((CHUNKS, LANES), F32)
+    for j in range(0, steps, 2):
+        pair, sizes = [], []
+        for i in (j, j + 1):
+            t = steps - 1 - i if branch == 0 else i
+            size = step_ref[branch, tile, t]
+            pair.append(left)
+            sizes.append(size)
+            left = left + size
+        low = steps - 2 - j if branch == 0 else j
+        if branch == 0:
+            pair, sizes = pair[::-1], sizes[::-1]
+        spans = jnp.concatenate(pair, 0).astype(BF16)
+        drive = jnp.concatenate(sizes, 0).astype(BF16) * u_ref[branch, low * CHUNKS : (low + 2) * CHUNKS, cols]
+        for n in range(16):
+            at = ((low // 2) * 16 + n) * 16
+            part = jnp.exp2(rates[n] * spans) * (drive * in_half[branch, at : at + 16, :])
+            states[n] = part if states[n] is None else states[n] + part
+    total_ref[branch, tile] = left
+    for n in range(16):
+        state = states[n].astype(F32)
+        end_ref[branch, tile, n * CHUNKS : (n + 1) * CHUNKS, :] = state[:CHUNKS] + state[CHUNKS:]
 
 
 def device_state(branch, tile, rest_ref, end_ref, total_ref):
@@ -240,7 +277,7 @@
     x_hbm, conv_own, bias_own, proj_own, step_own, shift_own, rate_own, skip_own, result_ref,
     rows_ref, conv_in, bias_in, shift_in, rate_in, skip_in,
     conv_ref, proj_weight_ref, rest_ref, step_weight_ref,
-    u_ref, rows_f32, in_wide, out_wide, out_half, step_ref, y_ref, end_ref, total_ref, chunk_carry,
+    u_ref, rows_f32, in_wide, out_wide, in_half, out_half, step_ref, y_ref, end_ref, total_ref, chunk_carry,
     mine_state, mine_time, out0, in0, out1, in1, out2, in2, out3, in3, out4, in4, own_carry,
     local_state, local_time,
     local_sem, halo_send, halo_recv, gather_send, gather_recv,
@@ -258,6 +295,8 @@
     right = (s + lax.div(y + 1, 4) * flip, y_right * 2 + core)
     left = (s + (1 - lax.div(y + 3, 4)) * flip, y_left * 2 + core)
     sibling = (s, y * 2 + other)
+    right_far = (s + lax.div(y + 2, 4) * flip, y_far * 2 + core)
+    left_far = (s + (1 - lax.div(y + 2, 4)) * flip, y_far * 2 + core)
     place = s * grp + g
     count = seq * grp
     after, before = lax.rem(place + 1, count), lax.rem(place + count - 1, count)
@@ -297,7 +336,7 @@
     def greet(device):
         pl.semaphore_signal(barrier, inc=1, device_id=device, device_id_type=MESH)
 
-    for device in (right, left, after, before, sibling):
+    for device in (right, left, right_far, left_far, after, before, sibling):
         greet(device)
     for d in range(1, chips):
         greet(chip_at(lax.rem(chip + d, chips)))
@@ -316,7 +355,7 @@
     rest_ref[g, 4:8, :] = jnp.zeros((4, width), F32)
     rest_ref[g, 8:24, :] = rate_in[0] * -LOG2E
     rest_ref[g, 24:40, :] = rate_in[1] * -LOG2E
-    pl.semaphore_wait(barrier, 5 + chips - 1 + groups - 1)
+    pl.semaphore_wait(barrier, 7 + chips - 1 + groups - 1)
 
     halos = [
         remote(x_hbm.at[rows - HALO : rows], rows_ref.at[0:HALO], halo_send.at[0], halo_recv.at[0], after),
@@ -325,16 +364,18 @@
             halo_recv.at[1], before,
         ),
     ]
-    whole = (conv_ref, proj_weight_ref, rest_ref, step_weight_ref)
-    own = (conv_ref.at[g], proj_own, rest_ref.at[g], step_own)
-    cuts = ((0, 8, 16), None, (0, 24, 40), None)
+    whole = (conv_ref, proj_weight_ref, rest_ref, step_weight_ref, proj_weight_ref, step_weight_ref)
+    own = (
+        conv_ref.at[g], proj_own.at[0], rest_ref.at[g], step_own.at[0], proj_own.at[1], step_own.at[1]
+    )
+    branch_of = (None, 0, None, 0, 1, 1)
+    cuts = ((0, 8, 16), (0, 80, 160), (0, 24, 40), (0, 64, 128), (0, 80, 160), (0, 64, 128))
 
     def part(kind, slot, half):
-        if half is None:
-            return whole[kind].at[slot]
-        if cuts[kind] is not None:
-            return whole[kind].at[slot, cuts[kind][half] : cuts[kind][half + 1]]
-        return whole[kind].at[slot, half]
+        low, high = (0, cuts[kind][2]) if half is None else cuts[kind][half : half + 2]
+        if branch_of[kind] is None:
+            return whole[kind].at[slot, low:high]
+        return whole[kind].at[slot, branch_of[kind], low:high]
 
     sent_slot = (g, g, y_left * 2 + core, y_right * 2 + core, g, y_left * 2 + core,
                  y_right * 2 + core, y_far * 2 + core, y_far * 2 + core)
@@ -345,25 +386,33 @@
     targets = (right, left, right, left) + (sibling,) * 5
 
     def outgoing(kind, way):
-        dst = part(kind, sent_slot[way], halves[way])
-        src = own[kind] if way in (0, 1, 4) else dst
-        return remote(src, dst, gather_send.at[kind, way], gather_recv.at[kind, way], targets[way])
+        target = targets[way]
+        if kind in DIRECT and way in (2, 3):
+            dst = part(kind, g, halves[way])
+            src = own_part(kind, halves[way])
+            target = right_far if way == 2 else left_far
+        else:
+            dst = part(kind, sent_slot[way], halves[way])
+            src = own[kind] if way in (0, 1, 4) else dst
+        return remote(src, dst, gather_send.at[kind, way], gather_recv.at[kind, way], target)
 
     def arrived(kind, way):
         dst = part(kind, got_slot[way], halves[way])
         remote(dst, dst, gather_send.at[kind, way], gather_recv.at[kind, way], targets[way]).wait_recv()
 
+    def own_part(kind, half):
+        return own[kind].at[cuts[kind][half] : cuts[kind][half + 1]]
+
     def send_own(kind):
-        for way in (0, 1, 4):
+        for way in (0, 1, 2, 3, 4) if kind in DIRECT else (0, 1, 4):
             outgoing(kind, way).start()
 
     def forward_near(kind):
-        arrived(kind, 0)
-        outgoing(kind, 2).start()
-        outgoing(kind, 5).start()
-        arrived(kind, 1)
-        outgoing(kind, 3).start()
-        outgoing(kind, 6).start()
+        for way in (0, 1):
+            arrived(kind, way)
+            if kind not in DIRECT:
+                outgoing(kind, 2 + way).start()
+            outgoing(kind, 5 + way).start()
 
     def forward_far(kind):
         arrived(kind, 2)
@@ -402,47 +451,48 @@
     arrived(0, 8)
     conv_chip(y_far)
 
-    def project(at, totals):
-        new = []
-        for branch in range(2):
-            total = totals[branch]
-            for i in range(2):
-                shard = at * 2 + i
-                cols = pl.ds(pl.multiple_of(shard * width, width), width)
-                total = total + dot_t(u_ref[branch, :, cols], proj_weight_ref[shard, branch])
-            new.append(total)
-        return new
-
-    forward_near(1)
-    send_own(2)
-    send_own(3)
-    proj_copy.wait()
-    arrived(1, 4)
-    totals = [jnp.zeros((rows, proj_weight_ref.shape[2]), F32)] * 2
-    totals = project(y, totals)
-    arrived(1, 5)
-    totals = project(y_left, totals)
-    forward_far(1)
-    arrived(1, 6)
-    totals = project(y_right, totals)
-    arrived(1, 7)
-    arrived(1, 8)
-    totals = project(y_far, totals)
-    lows = []
-    for branch in range(2):
-        projected = totals[branch].astype(BF16)
-        spread_maps(branch, projected[:, 128:160], in_wide, out_wide, out_half)
-        lows.append(projected[:, 0:128])
+    lows = [None, None]
+
+    def project(branch, at, total):
+        for i in range(2):
+            shard = at * 2 + i
+            cols = pl.ds(pl.multiple_of(shard * width, width), width)
+            total = total + dot_t(u_ref[branch, :, cols], proj_weight_ref[shard, branch])
+        return total
+
+    def project_all(branch, kind):
+        arrived(kind, 4)
+        total = project(branch, y, jnp.zeros((rows, proj_weight_ref.shape[2]), F32))
+        arrived(kind, 5)
+        total = project(branch, y_left, total)
+        if kind == 1:
+            forward_far(kind)
+        arrived(kind, 6)
+        total = project(branch, y_right, total)
+        arrived(kind, 7)
+        arrived(kind, 8)
+        projected = project(branch, y_far, total).astype(BF16)
+        spread_maps(branch, projected[:, 128:160], in_wide, out_wide, in_half, out_half)
+        lows[branch] = projected[:, 0:128]
 
     def steps_of(branch, at):
         for i in range(2):
             step_sizes(branch, at * 2 + i, lows[branch], step_weight_ref, rest_ref, step_ref)
 
-    def scan(branch, at):
+    def scan(branch, at, start=0, stop=tiles_chip):
         def body(i, _):
             scan_tile(
                 branch, at * tiles_chip + i, u_ref, rest_ref, step_ref, in_wide, out_wide, y_ref,
                 end_ref, total_ref, branch == 0,
+            )
+            return 0
+
+        lax.fori_loop(start, stop, body, 0)
+
+    def states_of(branch, at):
+        def body(i, _):
+            chunk_states(
+                branch, at * tiles_chip + i, u_ref, rest_ref, step_ref, in_half, end_ref, total_ref
             )
             return 0
 
@@ -587,62 +637,86 @@
 
         lax.fori_loop(start // 2, stop // 2, body, 0)
 
+    forward_near(1)
+    send_own(2)
+    send_own(3)
+    proj_copy.wait()
+    project_all(0, 1)
+
     step_copy.wait()
     arrived(2, 4)
     arrived(3, 4)
     steps_of(0, y)
+    forward_near(2)
+    forward_near(3)
+    send_own(4)
+    send_own(5)
     scan(0, y)
     finish(0, y)
-    forward_near(2)
-    forward_near(3)
-    steps_of(1, y)
-    relay(0, y)
-    scan(1, y)
-    finish(1, y)
     arrived(2, 5)
     arrived(3, 5)
     steps_of(0, y_left)
-    relay(1, y)
+    forward_far(2)
+    forward_far(3)
+    relay(0, y)
     scan(0, y_left)
     finish(0, y_left)
-    forward_far(2)
-    forward_far(3)
     arrived(2, 6)
     arrived(3, 6)
     steps_of(0, y_right)
     relay(0, y_left)
-    scan(0, y_right)
+    scan(0, y_right, 0, 4)
+    forward_near(4)
+    scan(0, y_right, 4, 8)
     finish(0, y_right)
     for kind in (2, 3):
         for way in (7, 8):
             arrived(kind, way)
     steps_of(0, y_far)
     relay(0, y_right)
-    scan(0, y_far)
+    scan(0, y_far, 0, 4)
+    forward_near(5)
+    forward_far(4)
+    scan(0, y_far, 4, 8)
     finish(0, y_far)
+    project_all(1, 4)
+    relay(0, y_far)
+    arrived(5, 4)
+    steps_of(1, y)
+    forward_far(5)
+    states_of(1, y)
+    finish(1, y)
+    arrived(5, 5)
     steps_of(1, y_left)
-    relay(0, y_far)
-    scan(1, y_left)
+    relay(1, y)
+    states_of(1, y_left)
     finish(1, y_left)
-    combine_chips(0)
+    arrived(5, 6)
     steps_of(1, y_right)
     relay(1, y_left)
-    scan(1, y_right)
+    states_of(1, y_right)
     finish(1, y_right)
-    combine_groups(0)
+    combine_chips(0)
+    arrived(5, 7)
+    arrived(5, 8)
     steps_of(1, y_far)
     relay(1, y_right)
+    states_of(1, y_far)
+    finish(1, y_far)
+    scan(1, y, 0, 4)
+    relay(1, y_far)
+    scan(1, y, 4, 8)
+    scan(1, y_left)
+    combine_groups(0)
+    scan(1, y_right, 0, 4)
+    combine_chips(1)
+    scan(1, y_right, 4, 8)
     scan(1, y_far)
-    finish(1, y_far)
     receive(0)
-    relay(1, y_far)
-    correct(0, True, 0, 8)
-    combine_chips(1)
-    correct(0, True, 8, 16)
+    correct(0, True, 0, 16)
+    combine_groups(1)
     back_to_core(0).wait_recv()
-    correct(0, False, 0, 8)
-    combine_groups(1)
-    correct(0, False, 8, 16)
+    correct(0, False, 0, 16)
     receive(1)
     correct(1, True, 0, 16)
     back_to_core(1).wait_recv()
@@ -650,7 +724,7 @@
 
     for copy in halos:
         copy.wait_send()
-    for kind in range(4):
+    for kind in range(6):
         for way in range(9):
             outgoing(kind, way).wait_send()
     for branch in range(2):
@@ -701,6 +775,7 @@
             vmem((2, rows * 16, LANES), F32),
             vmem((2, rows * 16, LANES), F32),
             vmem((2, rows * 16, LANES), BF16),
+            vmem((2, rows * 16, LANES), BF16),
             vmem((2, tiles, steps, CHUNKS, LANES), F32),
             vmem((tiles, steps, CHUNKS, LANES), F32),
             vmem((2, tiles, 16 * CHUNKS, LANES), F32),
@@ -724,8 +799,8 @@
             dma((8,)),
             dma((2,)),
             dma((2,)),
-            dma((4, 9)),
-            dma((4, 9)),
+            dma((6, 9)),
+            dma((6, 9)),
             dma((2, 4)),
             dma((2, 4)),
             dma((2, chips)),

time: 105 us -> 94.5 us (0.900)
  Pallas kernels: 102 us -> 91.5 us
    pallas_call x1, Pallas kernels: 102 us -> 91.5 us  [run_whole(): pl.pallas_call(whole_kernel, out_shape=jax.ShapeDtypeStruct((rows, channe...]
where the time goes in v4:
time: 94.5 us; the launch traced here: 94.3 us
  Pallas kernels  91.5 us (97%)
  other arithmetic  2.83 us (3%)
    pallas_call x1, Pallas kernels, run_whole(): pl.pallas_call(whole_kernel, out_shape=jax.ShapeDtypeStruct((rows, channe...  91.5 us
    convert_element_type x1, other arithmetic, local(): (mixed.astype(F32) * jax.nn.silu(inner_gate.astype(F32))).astype(BF16)  2.83 us

profile of v4, /device:TPU:1, one launch (start us, length us, event | category | flops | bytes accessed | tf_op | source)
XLA Modules:
  0.0 94.3 jit_solution(11806520047802478044)
XLA Ops:
  0.0 0.0 copy-start
  0.0 91.5 %shard_map.91 = bf16[128,4096]{1,0:T(8,128)(2,1)} custom-call(bf16[128,4096]{1,0:T(8,128)(2,1)} %x_hbm.1, f32[2,4,512]{2,1,0:T(4,128)} %conv_own.1, f32[2,512]{1,0:T(2,128)} %bias_own.1, bf16[2,160,512]{2,1,0:T(8,128)(2,1)} %bitcast.1, bf16[2,128,512]{2,1,0:T(8,128)(2,1)} %step_own.1, f32[2,512]{1,0:T(2,128)} %shift_own.1, f32[2,16,512]{2,1,0:T(8,128)} %rate_own.1, ...), custom_call_target="tpu_custom_call" | custom-call | tf_op jit(solution)/shard_map/pallas_call | solution.py:757
  91.5 0.0 copy-done
  91.5 2.8 %fusion.4 = bf16[128,4096]{1,0:T(8,128)(2,1)} fusion(bf16[128,4096]{1,0:T(8,128)(2,1)S(1)} %copy-done, bf16[128,4096]{1,0:T(8,128)(2,1)} %shard_map.91), kind=kLoop, calls=%fused_computation.6 | loop fusion | flops 4194304 | bytes 3145728 | tf_op jit(solution)/shard_map/convert_element_type | solution.py:836
Async XLA Ops:
  0.0 91.5 %copy-start = (bf16[128,4096]{1,0:T(8,128)(2,1)S(1)}, bf16[128,4096]{1,0:T(8,128)(2,1)}, u32[]{:S(2)}) copy-start(bf16[128,4096]{1,0:T(8,128)(2,1)} %param.10) | copy-start | bytes 3145732

commit v5 on v4

--- a/solution.py
+++ b/solution.py
@@ -220,22 +220,28 @@
     return values[0:16], values[16:17] + values[17:18]
 
 
-def correct_tile(
-    branch, tile, rest_ref, step_ref, end_ref, out_half, carry, y_ref, total_ref, chunk_carry
-):
+def chunk_carries(branch, tile, rest_ref, end_ref, carry, total_ref):
     shard, column = lax.div(tile, 4), lax.rem(tile, 4)
     lanes = pl.ds(pl.multiple_of(column * LANES, LANES), LANES)
     first = ROW_RATE + 16 * branch
-    steps = step_ref.shape[2]
     rates = rest_ref[shard, first : first + 16, lanes]
+    carries = []
     for j in range(CHUNKS):
         k = j if branch == 0 else CHUNKS - 1 - j
-        chunk_carry[pl.ds(k, 16, stride=CHUNKS), :] = carry
+        carries.append((k, carry))
         if j < CHUNKS - 1:
             carry = (
                 jnp.exp2(rates * total_ref[branch, tile, k : k + 1, :]) * carry
                 + end_ref[branch, tile, pl.ds(k, 16, stride=CHUNKS), :]
             )
+    return carries
+
+
+def correct_tile(branch, tile, rest_ref, step_ref, out_half, y_ref, chunk_carry):
+    shard, column = lax.div(tile, 4), lax.rem(tile, 4)
+    lanes = pl.ds(pl.multiple_of(column * LANES, LANES), LANES)
+    first = ROW_RATE + 16 * branch
+    steps = step_ref.shape[2]
     entering = []
     wide = []
     for n in range(16):
@@ -281,7 +287,7 @@
     mine_state, mine_time, out0, in0, out1, in1, out2, in2, out3, in3, out4, in4, own_carry,
     local_state, local_time,
     local_sem, halo_send, halo_recv, gather_send, gather_recv,
-    send0, recv0, send1, recv1, send2, recv2, send3, recv3, send4, recv4,
+    send0, recv0, send1, recv1, send2, recv2, send3, recv3, send4, recv4, known,
 ):
     s, g = lax.axis_index("seq"), lax.axis_index("grp")
     seq, grp = lax.axis_size("seq"), lax.axis_size("grp")
@@ -340,8 +346,12 @@
         greet(device)
     for d in range(1, chips):
         greet(chip_at(lax.rem(chip + d, chips)))
-    for d in range(1, groups):
-        greet(group_at(lax.rem(group + d, groups)))
+    high = lax.rem(group, 2)
+    next_group = group_at(lax.rem(group + 2, groups))
+    last_group = group_at(lax.rem(group + groups - 2, groups))
+    high_group = group_at(group + 1 - 2 * high)
+    for device in (next_group, last_group, high_group):
+        greet(device)
 
     for copy in small_copies:
         copy.wait()
@@ -355,7 +365,16 @@
     rest_ref[g, 4:8, :] = jnp.zeros((4, width), F32)
     rest_ref[g, 8:24, :] = rate_in[0] * -LOG2E
     rest_ref[g, 24:40, :] = rate_in[1] * -LOG2E
-    pl.semaphore_wait(barrier, 7 + chips - 1 + groups - 1)
+    pl.semaphore_wait(barrier, 10 + chips - 1)
+
+    def pass_on(turn):
+        for device in (next_group, last_group) if turn < 3 else (high_group,):
+            pl.semaphore_signal(known.at[turn], inc=1, device_id=device, device_id_type=MESH)
+
+    def learn(turn):
+        pl.semaphore_wait(known.at[turn], 2 if turn < 3 else 1)
+
+    pass_on(0)
 
     halos = [
         remote(x_hbm.at[rows - HALO : rows], rows_ref.at[0:HALO], halo_send.at[0], halo_recv.at[0], after),
@@ -442,11 +461,15 @@
         copy.wait_recv()
     arrived(0, 4)
     conv_chip(y)
+    learn(0)
+    pass_on(1)
     arrived(0, 5)
     conv_chip(y_left)
     forward_far(0)
     arrived(0, 6)
     conv_chip(y_right)
+    learn(1)
+    pass_on(2)
     arrived(0, 7)
     arrived(0, 8)
     conv_chip(y_far)
@@ -506,15 +529,20 @@
         )
 
     def finish(branch, at):
-        for i in range(4):
-            k = at * 4 + i
-            state, elapsed = device_state(branch, 2 * k + core, rest_ref, end_ref, total_ref)
-            mine_state[branch, k] = state
-            mine_time[branch, k] = jnp.broadcast_to(elapsed, (8, LANES))
-            out0[branch, k] = as_message(
-                *device_state(branch, 2 * k + other, rest_ref, end_ref, total_ref)
-            )
+        span = range(4)
+        mine = [
+            device_state(branch, 2 * (at * 4 + i) + core, rest_ref, end_ref, total_ref) for i in span
+        ]
+        theirs = [
+            as_message(*device_state(branch, 2 * (at * 4 + i) + other, rest_ref, end_ref, total_ref))
+            for i in span
+        ]
+        for i in span:
+            out0[branch, at * 4 + i] = theirs[i]
         to_core(branch, at).start()
+        for i in span:
+            mine_state[branch, at * 4 + i] = mine[i][0]
+            mine_time[branch, at * 4 + i] = jnp.broadcast_to(mine[i][1], (8, LANES))
 
     def rates_of(branch, k):
         tile = 2 * k + core
@@ -539,11 +567,14 @@
 
     def relay(branch, at):
         to_core(branch, at).wait_recv()
+        messages = []
         for i in range(4):
             k = at * 4 + i
             state1, time1, state2, time2 = in_order(branch, k)
             state = jnp.exp2(rates_of(branch, k) * time2) * state1 + state2
-            out1[branch, k] = as_message(state, time1 + time2)
+            messages.append(as_message(state, time1 + time2))
+        for i in range(4):
+            out1[branch, at * 4 + i] = messages[i]
         for i in range(4):
             k = at * 4 + i
 
@@ -561,10 +592,10 @@
         rates = rates_of(branch, chip)
         state = jnp.zeros((16, LANES), F32)
         elapsed = jnp.zeros((1, LANES), F32)
+        entering = []
         for j in range(chips):
             k = j if branch == 0 else chips - 1 - j
-            local_state[branch, k] = state
-            local_time[branch, k] = jnp.broadcast_to(elapsed, (8, LANES))
+            entering.append((k, state, elapsed))
             gained, span = of_message(in1[branch, k])
             state = jnp.exp2(rates * span) * state + gained
             elapsed = elapsed + span
@@ -575,6 +606,9 @@
                 out2.at[branch], in2.at[branch, group], send2.at[branch, k], recv2.at[branch, group],
                 group_at(k),
             ).start()
+        for k, state, elapsed in entering:
+            local_state[branch, k] = state
+            local_time[branch, k] = jnp.broadcast_to(elapsed, (8, LANES))
 
     def combine_groups(branch):
         for d in range(1, groups):
@@ -612,25 +646,34 @@
             ).wait_recv()
         in3[branch, chip] = out3[branch, chip]
         leads = core == branch
-        for k in range(chips):
-            carry = in3[branch, k].astype(F32)
-            state1, time1, _, _ = in_order(branch, k)
-            second = jnp.exp2(rates_of(branch, k) * time1) * carry + state1
-            own_carry[branch, k] = jnp.where(leads, carry, second).astype(BF16)
-            out4[branch, k] = jnp.where(leads, second, carry).astype(BF16)
+        for low in range(0, chips, 4):
+            pairs = []
+            for k in range(low, low + 4):
+                carry = in3[branch, k].astype(F32)
+                state1, time1, _, _ = in_order(branch, k)
+                second = jnp.exp2(rates_of(branch, k) * time1) * carry + state1
+                pairs.append((jnp.where(leads, carry, second), jnp.where(leads, second, carry)))
+            for k in range(low, low + 4):
+                own_carry[branch, k] = pairs[k - low][0].astype(BF16)
+                out4[branch, k] = pairs[k - low][1].astype(BF16)
         back_to_core(branch).start()
 
     def correct(branch, mine, start, stop):
         held = own_carry if mine else in4
 
         def body(i, _):
-            for q in range(2):
-                k = 2 * i + q
-                tile = 2 * k + (core if mine else other)
-                correct_tile(
-                    branch, tile, rest_ref, step_ref, end_ref, out_half, held[branch, k].astype(F32),
-                    y_ref, total_ref, chunk_carry.at[q],
+            places = [(q, 2 * (2 * i + q) + (core if mine else other)) for q in range(2)]
+            carries = [
+                chunk_carries(
+                    branch, tile, rest_ref, end_ref, held[branch, 2 * i + q].astype(F32), total_ref
                 )
+                for q, tile in places
+            ]
+            for q, tile in places:
+                for k, carry in carries[q]:
+                    chunk_carry[q, pl.ds(k, 16, stride=CHUNKS), :] = carry
+            for q, tile in places:
+                correct_tile(branch, tile, rest_ref, step_ref, out_half, y_ref, chunk_carry.at[q])
                 if branch == 1:
                     mix_tile(tile, y_ref, result_ref, rows_f32.at[q])
             return 0
@@ -642,6 +685,8 @@
     send_own(3)
     proj_copy.wait()
     project_all(0, 1)
+    learn(2)
+    pass_on(3)
 
     step_copy.wait()
     arrived(2, 4)
@@ -652,6 +697,7 @@
     send_own(4)
     send_own(5)
     scan(0, y)
+    learn(3)
     finish(0, y)
     arrived(2, 5)
     arrived(3, 5)
@@ -811,6 +857,7 @@
             dma((2, chips)),
             dma((2,)),
             dma((2,)),
+            pltpu.SemaphoreType.REGULAR((4,)),
         ],
         compiler_params=pltpu.CompilerParams(
             vmem_limit_bytes=56 << 20, collective_id=0, has_side_effects=True

time: 94.5 us -> 91.3 us (0.966)
  Pallas kernels: 91.5 us -> 88.3 us
    pallas_call x1, Pallas kernels: 91.5 us -> 88.3 us  [run_whole(): pl.pallas_call(whole_kernel, out_shape=jax.ShapeDtypeStruct((rows, channe...]
where the time goes in v5:
time: 91.3 us; the launch traced here: 91.1 us
  Pallas kernels  88.3 us (97%)
  other arithmetic  2.83 us (3%)
    pallas_call x1, Pallas kernels, run_whole(): pl.pallas_call(whole_kernel, out_shape=jax.ShapeDtypeStruct((rows, channe...  88.3 us
    convert_element_type x1, other arithmetic, local(): (mixed.astype(F32) * jax.nn.silu(inner_gate.astype(F32))).astype(BF16)  2.83 us

profile of v5, /device:TPU:1, one launch (start us, length us, event | category | flops | bytes accessed | tf_op | source)
XLA Modules:
  0.0 91.1 jit_solution(13935111543697937936)
XLA Ops:
  0.0 0.0 copy-start
  0.0 88.3 %shard_map.91 = bf16[128,4096]{1,0:T(8,128)(2,1)} custom-call(bf16[128,4096]{1,0:T(8,128)(2,1)} %x_hbm.1, f32[2,4,512]{2,1,0:T(4,128)} %conv_own.1, f32[2,512]{1,0:T(2,128)} %bias_own.1, bf16[2,160,512]{2,1,0:T(8,128)(2,1)} %bitcast.1, bf16[2,128,512]{2,1,0:T(8,128)(2,1)} %step_own.1, f32[2,512]{1,0:T(2,128)} %shift_own.1, f32[2,16,512]{2,1,0:T(8,128)} %rate_own.1, ...), custom_call_target="tpu_custom_call" | custom-call | tf_op jit(solution)/shard_map/pallas_call | solution.py:803
  88.3 0.0 copy-done
  88.3 2.8 %fusion.4 = bf16[128,4096]{1,0:T(8,128)(2,1)} fusion(bf16[128,4096]{1,0:T(8,128)(2,1)S(1)} %copy-done, bf16[128,4096]{1,0:T(8,128)(2,1)} %shard_map.91), kind=kLoop, calls=%fused_computation.6 | loop fusion | flops 4194304 | bytes 3145728 | tf_op jit(solution)/shard_map/convert_element_type | solution.py:883
Async XLA Ops:
  0.0 88.3 %copy-start = (bf16[128,4096]{1,0:T(8,128)(2,1)S(1)}, bf16[128,4096]{1,0:T(8,128)(2,1)}, u32[]{:S(2)}) copy-start(bf16[128,4096]{1,0:T(8,128)(2,1)} %param.10) | copy-start | bytes 3145732
